TPU v7x, 256 devices: a whole 4x4x8 slice. The times are simulated.
256 devices in a mesh: space: 16 (over z, x_hi), tm: 16 (over x_lo, y, core).
Axes of the slice: x: 4 (x_hi: 2, x_lo: 2; x = x_hi * 2 + x_lo), y: 4, z: 8, core: 2. Of those that a mesh axis runs over, the one named last changes fastest.
Arguments:
- snapshots: float32 [32768, 16384], P('space', 'tm'), may hold values from -3000 to 3000, as said below
- sketch: float32 [16384, 256], P('tm'), may hold values from -6 to 6
Outputs:
- refined: float32 [32768, 256], P('space')
- cosample: float32 [16384, 256], P('tm')
Inputs may be any that keep to these rules, and one draw needn't show every extreme that they name: `snapshots`: float32 snapshot values.
All inputs are finite; a program needn't handle non-finite values.
Results may differ from a plain program's by a relative error of at most 0.000071.
Values sent between devices are 32-bit elements; how exact they have to be, the bound alone decides.
A program may use at most 64 MiB of HBM per device.

v0:
```python
import jax
import jax.numpy as jnp
from jax import lax
from jax.sharding import PartitionSpec as P

EPS = 1e-06


def in_blocks(x, dim, peers):
    before, after = (x.shape[:dim], x.shape[dim + 1 :])
    return jnp.moveaxis(x.reshape(*before, peers, -1, *after), dim, 0)


def sent_and_summed(x, axis, dim):
    parts = in_blocks(x, dim, lax.axis_size(axis))
    arrived = lax.all_to_all(parts, axis, split_axis=0, concat_axis=0, tiled=True)
    return arrived.sum(axis=0)


def laid_out(parts, dim):
    parts = jnp.moveaxis(parts, 0, dim)
    shape = parts.shape
    return parts.reshape(*shape[:dim], shape[dim] * shape[dim + 1], *shape[dim + 2 :])


def from_everyone(x, axis):
    copies = jnp.broadcast_to(x, (lax.axis_size(axis), *x.shape))
    return lax.all_to_all(copies, axis, split_axis=0, concat_axis=0, tiled=True)


def gather_directly(x, axis, dim):
    return laid_out(from_everyone(x, axis), dim)


def scale_rows(value):
    return value * lax.rsqrt(jnp.mean(value * value, axis=1, keepdims=True) + EPS)


def forward(block, right):
    return jnp.dot(
        block, right, precision=lax.Precision.HIGHEST, preferred_element_type=jnp.float32
    )


def backward(block, right):
    return lax.dot_general(
        block,
        right,
        (((0,), (0,)), ((), ())),
        precision=lax.Precision.HIGHEST,
        preferred_element_type=jnp.float32,
    )


def local(snapshots, sketch):
    owned = scale_rows(sent_and_summed(forward(snapshots, sketch), "tm", 0))
    sample = gather_directly(owned, "tm", 0)
    owned_times = scale_rows(sent_and_summed(backward(snapshots, sample), "space", 0))
    cosample = gather_directly(owned_times, "space", 0)
    owned_refined = scale_rows(sent_and_summed(forward(snapshots, cosample), "tm", 0))
    refined = gather_directly(owned_refined, "tm", 0)
    return (refined, cosample)


def solution(mesh):
    return jax.shard_map(
        local,
        mesh=mesh,
        in_specs=(P("space", "tm"), P("tm", None)),
        out_specs=(P("space", None), P("tm", None)),
        check_vma=False,
    )
```

profile of v0, /device:TPU:1, one launch (start us, length us, event | category | flops | bytes accessed | tf_op | source)
XLA Modules:
  0.0 240.1 jit_solution(13538778049770539701)
XLA Ops:
  0.6 0.0 copy-start
  0.6 1.2 copy-done
  1.9 9.0 %fusion = f32[2048,256]{1,0:T(8,128)S(1)} fusion(f32[2048,1024]{1,0:T(8,128)} %param.2, f32[1024,256]{1,0:T(8,128)S(1)} %copy-done), kind=kOutput, calls=%fused_computation.12 | convolution fusion | flops 6442450944 | bytes 11534336 | tf_op jit(solution)/shard_map/dot_general | solution.py:40
  10.9 33.4 %all_to_all.30 = f32[16,128,256]{2,1,0:T(8,128)S(1)} all-to-all(f32[16,128,256]{2,1,0:T(8,128)S(1)} %bitcast.19), channel_id=1, replica_groups=mesh['space'=16,'tm'=16] {'tm'}, dimensions={0} | all-to-all | bytes 4194304 | tf_op jit(solution)/shard_map/all_to_all | solution.py:16
  44.3 0.1 reduce_sum.54
  44.4 0.1 multiply_reduce_fusion.1
  44.5 0.1 broadcast_multiply_fusion.1
  44.6 0.2 broadcast_in_dim.12
  44.8 30.4 %all_to_all.31 = f32[16,128,256]{2,1,0:T(8,128)S(1)} all-to-all(f32[16,128,256]{2,1,0:T(8,128)S(1)} %broadcast_in_dim.12), channel_id=1, replica_groups=mesh['space'=16,'tm'=16] {'tm'}, dimensions={0} | all-to-all | bytes 4194304 | tf_op jit(solution)/shard_map/all_to_all | solution.py:28
  75.2 9.6 %convolution_bitcast_fusion.1 = f32[1024,256]{0,1:T(8,128)S(1)} fusion(f32[2048,256]{1,0:T(8,128)S(1)} %bitcast.24, f32[2048,1024]{1,0:T(8,128)} %param.2), kind=kOutput, calls=%fused_computation.2 | convolution fusion | flops 6442450944 | bytes 11534336 | tf_op jit(solution)/shard_map/dot_general | solution.py:46
  84.8 0.3 copy.9
  85.1 38.5 %all_to_all.32 = f32[16,64,256]{2,1,0:T(8,128)S(1)} all-to-all(f32[16,64,256]{2,1,0:T(8,128)S(1)} %bitcast.25), channel_id=1, replica_groups=mesh['space'=16,'tm'=16] {'space'}, dimensions={0} | all-to-all | bytes 2097152 | tf_op jit(solution)/shard_map/all_to_all | solution.py:16
  123.6 0.1 reduce_sum.56
  123.7 0.1 multiply_reduce_fusion.2
  123.8 0.1 broadcast_multiply_fusion.2
  123.9 0.1 broadcast_in_dim.13
  124.0 32.2 %all_to_all.33 = f32[16,64,256]{2,1,0:T(8,128)S(1)} all-to-all(f32[16,64,256]{2,1,0:T(8,128)S(1)} %broadcast_in_dim.13), channel_id=1, replica_groups=mesh['space'=16,'tm'=16] {'space'}, dimensions={0} | all-to-all | bytes 2097152 | tf_op jit(solution)/shard_map/all_to_all | solution.py:28
  156.2 15.8 %convolution_bitcast_fusion = f32[32,16,8,128]{3,2,1,0:T(8,128)S(1)} fusion(f32[1024,256]{1,0:T(8,128)S(1)} %bitcast.20, f32[2048,1024]{1,0:T(8,128)} %param.2), kind=kOutput, calls=%fused_computation.1 | convolution fusion | flops 6442450944 | bytes 11534336 | tf_op jit(solution)/shard_map/dot_general | solution.py:40
  172.0 0.2 copy.16
  172.2 33.2 %all_to_all.34 = f32[16,128,256]{1,2,0:T(8,128)} all-to-all(f32[16,128,256]{1,2,0:T(8,128)S(1)} %bitcast.22), channel_id=1, replica_groups=mesh['space'=16,'tm'=16] {'tm'}, dimensions={0} | all-to-all | bytes 4194304 | tf_op jit(solution)/shard_map/all_to_all | solution.py:16
  205.4 1.7 reduce_sum.58
  207.2 0.1 copy.12
  207.3 0.2 broadcast_in_dim.14
  207.5 30.4 %all_to_all.35 = f32[16,128,256]{2,1,0:T(8,128)S(1)} all-to-all(f32[16,128,256]{2,1,0:T(8,128)S(1)} %broadcast_in_dim.14), channel_id=1, replica_groups=mesh['space'=16,'tm'=16] {'tm'}, dimensions={0} | all-to-all | bytes 4194304 | tf_op jit(solution)/shard_map/all_to_all | solution.py:28
  237.9 1.3 copy.19
  239.2 1.0 copy.20
  (5 shorter events, 0.1 us)
Async XLA Ops:
  0.6 1.2 copy-start
where the time goes:
time: 241 us; the launch traced here: 240 us
  blocking collectives  198 us (82%)
  matrix products  34.5 us (14%)
  local copies, waits for them, and re-layouts  4.64 us (2%)
    all_to_all x3, blocking collectives, sent_and_summed(): lax.all_to_all(parts, axis, split_axis=0, concat_axis=0, tiled=True)  105 us
    all_to_all x3, blocking collectives, from_everyone(): return lax.all_to_all(copies, axis, split_axis=0, concat_axis=0, tiled=True)  92.9 us
    dot_general x2, matrix products, forward(): jnp.dot(block, right, precision=lax.Precision.HIGHEST, preferred_element_...  24.9 us
    dot_general x1, matrix products, backward(): lax.dot_general(block, right, (((0,), (0,)), ((), ())), precision=lax.Pre...  9.61 us

commit v1 on v0

v1 whole, which is shorter than its diff:
```python
import functools

import jax
import jax.numpy as jnp
from jax import lax
from jax.experimental import pallas as pl
from jax.experimental.pallas import tpu as pltpu
from jax.sharding import PartitionSpec as P

EPS = 1e-06
MESH = pl.DeviceIdType.MESH
F32, BF16 = jnp.float32, jnp.bfloat16
NZ, NY = 8, 4
N = 4
NB = 4


def split(value):
    high = value.astype(BF16)
    return high, (value - high.astype(F32)).astype(BF16)


def scale_rows(value):
    return value * lax.rsqrt(jnp.mean(value * value, axis=1, keepdims=True) + EPS)


def dot(a, b):
    return jnp.dot(a, b, preferred_element_type=F32)


def dot_t(a, b):
    return lax.dot_general(a, b, (((0,), (0,)), ((), ())), preferred_element_type=F32)


def kernel(
    snap_ref, sketch_ref, refined_ref, cosample_ref,
    wide, s_hi, s_lo, b_hi, b_lo, part, sample, p_hi, p_lo, back, c_hi, c_lo, last,
    from_core, from_y, from_x, from_x2, from_y2, from_xh, from_z,
    load_sem, send_sem, recv_sem, send_sem_b, recv_sem_b,
):
    points, times = wide.shape
    space, tm = lax.axis_index("space"), lax.axis_index("tm")
    z, xh = space // 2, lax.rem(space, 2)
    xl, y, core = tm // 8, lax.rem(tm // 2, 4), lax.rem(tm, 2)

    def at_tm(xl, y, core):
        return {"space": space, "tm": xl * 8 + y * 2 + core}

    def at_space(z, xh):
        return {"space": z * 2 + xh, "tm": tm}

    other_core, other_x = at_tm(xl, y, 1 - core), at_tm(1 - xl, y, core)
    other_xh = at_space(z, 1 - xh)
    y_at = [lax.rem(y + d, NY) for d in range(NY)]
    z_at = [lax.rem(z + d, NZ) for d in range(NZ)]
    peer_y = [at_tm(xl, y_at[d], core) for d in range(NY)]
    peer_z = [at_space(z_at[d], xh) for d in range(NZ)]

    chunk = points // N
    width = times // NB

    def load(i):
        rows = pl.ds(pl.multiple_of(i * chunk, chunk), chunk)
        return pltpu.make_async_copy(snap_ref.at[rows], wide.at[rows], load_sem.at[i])

    for i in range(N):
        load(i).start()

    barrier = pltpu.get_barrier_semaphore()
    peers = [other_core, other_x, other_xh, *peer_y[1:], *peer_z[1:]]
    for peer in peers:
        pl.semaphore_signal(barrier, inc=1, device_id=peer, device_id_type=MESH)

    b_hi[...], b_lo[...] = split(sketch_ref[...])
    back[...] = jnp.zeros_like(back)
    last[...] = jnp.zeros_like(last)
    pl.semaphore_wait(barrier, len(peers))

    def send(src, dst, sent, arrived, peer):
        pltpu.make_async_remote_copy(
            src_ref=src, dst_ref=dst, send_sem=sent, recv_sem=arrived, device_id=peer, device_id_type=MESH
        ).start()

    def take(rows, sem):
        ref = part.at[pl.ds(0, rows)]
        pltpu.make_async_copy(ref, ref, sem).wait()

    def rows_of(start, size):
        return pl.ds(pl.multiple_of(start, 8), size)

    half = chunk // 2
    sub = half // 2

    def tm_stages(phase, multiply, summed, gathered):
        sent, got = send_sem.at[phase], recv_sem.at[phase]

        def mine(i):
            return i * chunk + core * half

        def first(i):
            multiply(i)
            src = rows_of(i * chunk + (1 - core) * half, half)
            send(summed.at[src], from_core.at[phase, i], sent.at[0], got.at[0, i], other_core)

        def over_1(i):
            take(half, got.at[0, i])
            a, b = mine(i), mine(i) + sub
            own = rows_of(a, half)
            summed[own, :] += from_core[phase, i]
            for d in (2, 1, 3):
                src = rows_of(a + y_at[d] * (sub // 4), sub // 4)
                send(summed.at[src], from_y.at[phase, i, d - 1], sent.at[1], got.at[1, i], peer_y[d])
            src = rows_of(b + (1 - xl) * (sub // 2), sub // 2)
            send(summed.at[src], from_x.at[phase, i], sent.at[1], got.at[1, i], other_x)

        def over_2(i):
            take(3 * (sub // 4) + sub // 2, got.at[1, i])
            a, b = mine(i) + y * (sub // 4), mine(i) + sub + xl * (sub // 2)
            own = rows_of(a, sub // 4)
            summed[own, :] += from_y[phase, i, 0] + from_y[phase, i, 1] + from_y[phase, i, 2]
            own = rows_of(b, sub // 2)
            summed[own, :] += from_x[phase, i]
            for d in (2, 1, 3):
                src = rows_of(b + y_at[d] * (sub // 8), sub // 8)
                send(summed.at[src], from_y2.at[phase, i, d - 1], sent.at[2], got.at[2, i], peer_y[d])
            src = rows_of(a + (1 - xl) * (sub // 8), sub // 8)
            send(summed.at[src], from_x2.at[phase, i], sent.at[2], got.at[2, i], other_x)

        def finish(i):
            take(4 * (sub // 8), got.at[2, i])
            a = rows_of(mine(i) + y * (sub // 4) + xl * (sub // 8), sub // 8)
            b = rows_of(mine(i) + sub + xl * (sub // 2) + y * (sub // 8), sub // 8)
            total = summed[b, :] + (from_y2[phase, i, 0] + from_y2[phase, i, 1] + from_y2[phase, i, 2])
            gathered[b, :] = scale_rows(total)
            for d in (2, 1, 3):
                send(gathered.at[b], gathered.at[b], sent.at[3], got.at[3, i], peer_y[d])
            gathered[a, :] = scale_rows(summed[a, :] + from_x2[phase, i])
            send(gathered.at[a], gathered.at[a], sent.at[3], got.at[3, i], other_x)

        def spread(i):
            take(4 * (sub // 8), got.at[3, i])
            a = rows_of(mine(i) + y * (sub // 4), sub // 4)
            b = rows_of(mine(i) + sub + xl * (sub // 2), sub // 2)
            for d in (2, 1, 3):
                send(gathered.at[a], gathered.at[a], sent.at[4], got.at[4, i], peer_y[d])
            send(gathered.at[b], gathered.at[b], sent.at[4], got.at[4, i], other_x)

        def to_core(i):
            take(3 * (sub // 4) + sub // 2, got.at[4, i])
            own = rows_of(mine(i), half)
            send(gathered.at[own], gathered.at[own], sent.at[5], got.at[5, i], other_core)

        def arrive(i):
            take(half, got.at[5, i])

        def close():
            for stage, rows in enumerate((half, 5 * (sub // 4), sub // 2, sub // 2, 5 * (sub // 4), half)):
                take(N * rows, sent.at[stage])

        return [first, over_1, over_2, finish, spread, to_core], arrive, close

    def space_stages(multiply):
        half = width // 2
        piece = half // NZ

        def first(j):
            multiply(j)
            src = rows_of(j * width + (1 - xh) * half, half)
            send(back.at[src], from_xh.at[j], send_sem_b.at[0], recv_sem_b.at[0, j], other_xh)

        def over(j):
            take(half, recv_sem_b.at[0, j])
            a = j * width + xh * half
            own = rows_of(a, half)
            back[own, :] += from_xh[j]
            for d in (4, 3, 5, 2, 6, 1, 7):
                src = rows_of(a + z_at[d] * piece, piece)
                send(back.at[src], from_z.at[j, d - 1], send_sem_b.at[1], recv_sem_b.at[1, j], peer_z[d])

        def finish(j):
            take(7 * piece, recv_sem_b.at[1, j])
            own = rows_of(j * width + xh * half + z * piece, piece)
            total = back[own, :]
            for d in range(1, NZ):
                total += from_z[j, d - 1]
            cosample_ref[own, :] = scale_rows(total)
            for d in (4, 3, 5, 2, 6, 1, 7):
                send(cosample_ref.at[own], cosample_ref.at[own], send_sem_b.at[2], recv_sem_b.at[2, j], peer_z[d])

        def spread(j):
            take(7 * piece, recv_sem_b.at[2, j])
            own = rows_of(j * width + xh * half, half)
            send(cosample_ref.at[own], cosample_ref.at[own], send_sem_b.at[3], recv_sem_b.at[3, j], other_xh)

        def arrive(j):
            take(half, recv_sem_b.at[3, j])

        def close():
            for stage, rows in enumerate((half, 7 * piece, 7 * piece, half)):
                take(NB * rows, send_sem_b.at[stage])

        return [first, over, finish, spread], arrive, close

    def run(stages, parts, steps):
        def step(t, _):
            for s in reversed(range(len(stages))):
                stage, count = stages[s], parts[s]

                @pl.when((t >= s) & (t < s + count))
                def _():
                    stage(t - s)

            return 0

        lax.fori_loop(0, steps, step, 0)

    def multiply_1(i):
        load(i).wait()

        def piece(q, _):
            rows = pl.ds(pl.multiple_of(i * chunk + q * 256, 256), 256)
            high, low = split(wide[rows, :])
            s_hi[rows, :] = high
            s_lo[rows, :] = low
            part[rows, :] = dot(high, b_hi[...]) + (dot(high, b_lo[...]) + dot(low, b_hi[...]))
            return 0

        lax.fori_loop(0, chunk // 256, piece, 0)

    def add_back(i, j):
        rows = pl.ds(pl.multiple_of(i * chunk, chunk), chunk)
        columns = pl.ds(pl.multiple_of(j * width, width), width)
        high, low = s_hi[rows, columns], s_lo[rows, columns]
        back[columns, :] += dot_t(high, p_hi[...]) + (dot_t(high, p_lo[...]) + dot_t(low, p_hi[...]))

    def split_sample(i):
        rows = pl.ds(pl.multiple_of(i * chunk, chunk), chunk)
        p_hi[...], p_lo[...] = split(sample[rows, :])

    stages, arrive_1, close_1 = tm_stages(0, multiply_1, part, sample)

    def use_sample(i):
        arrive_1(i)
        split_sample(i)
        lax.fori_loop(0, NB, lambda j, _: (add_back(i, j), 0)[1], 0)

    run([*stages, use_sample], [N] * 6 + [N - 1], N + 5)
    arrive_1(N - 1)
    split_sample(N - 1)

    def add_last(i, j):
        rows = pl.ds(pl.multiple_of(i * chunk, chunk), chunk)
        columns = pl.ds(pl.multiple_of(j * width, width), width)
        high, low = s_hi[rows, columns], s_lo[rows, columns]
        last[rows, :] += dot(high, c_hi[...]) + (dot(high, c_lo[...]) + dot(low, c_hi[...]))

    def split_cosample(j):
        rows = pl.ds(pl.multiple_of(j * width, width), width)
        c_hi[...], c_lo[...] = split(cosample_ref[rows, :])

    stages, arrive_b, close_b = space_stages(functools.partial(add_back, N - 1))

    def use_cosample(j):
        arrive_b(j)
        split_cosample(j)
        lax.fori_loop(0, N, lambda i, _: (add_last(i, j), 0)[1], 0)

    run([*stages, use_cosample], [NB] * 4 + [NB - 1], NB + 3)
    arrive_b(NB - 1)
    split_cosample(NB - 1)

    stages, arrive_2, close_2 = tm_stages(1, lambda i: add_last(i, NB - 1), last, refined_ref)
    run([*stages, arrive_2], [N] * 7, N + 6)
    close_1()
    close_b()
    close_2()


def local(snapshots, sketch):
    (points, times), k = snapshots.shape, sketch.shape[1]
    chunk, width = points // N, times // NB
    half = chunk // 2
    sub = half // 2
    vmem = pl.BlockSpec(memory_space=pltpu.VMEM)
    return pl.pallas_call(
        kernel,
        name="window",
        out_shape=[jax.ShapeDtypeStruct((points, k), F32), jax.ShapeDtypeStruct((times, k), F32)],
        in_specs=[pl.BlockSpec(memory_space=pl.ANY), vmem],
        out_specs=[vmem, vmem],
        scratch_shapes=[
            pltpu.VMEM((points, times), F32),
            pltpu.VMEM((points, times), BF16),
            pltpu.VMEM((points, times), BF16),
            pltpu.VMEM((times, k), BF16),
            pltpu.VMEM((times, k), BF16),
            pltpu.VMEM((points, k), F32),
            pltpu.VMEM((points, k), F32),
            pltpu.VMEM((chunk, k), BF16),
            pltpu.VMEM((chunk, k), BF16),
            pltpu.VMEM((times, k), F32),
            pltpu.VMEM((width, k), BF16),
            pltpu.VMEM((width, k), BF16),
            pltpu.VMEM((points, k), F32),
            pltpu.VMEM((2, N, half, k), F32),
            pltpu.VMEM((2, N, 3, sub // 4, k), F32),
            pltpu.VMEM((2, N, sub // 2, k), F32),
            pltpu.VMEM((2, N, sub // 8, k), F32),
            pltpu.VMEM((2, N, 3, sub // 8, k), F32),
            pltpu.VMEM((NB, width // 2, k), F32),
            pltpu.VMEM((NB, NZ - 1, width // 2 // NZ, k), F32),
            pltpu.SemaphoreType.DMA((N,)),
            pltpu.SemaphoreType.DMA((2, 6)),
            pltpu.SemaphoreType.DMA((2, 6, N)),
            pltpu.SemaphoreType.DMA((4,)),
            pltpu.SemaphoreType.DMA((4, NB)),
        ],
        compiler_params=pltpu.CompilerParams(
            collective_id=0, has_side_effects=True, vmem_limit_bytes=52 << 20
        ),
        cost_estimate=pl.CostEstimate(
            flops=18 * points * times * k, bytes_accessed=4 * points * times, transcendentals=0
        ),
    )(snapshots, sketch)


def solution(mesh):
    return jax.shard_map(
        local,
        mesh=mesh,
        in_specs=(P("space", "tm"), P("tm", None)),
        out_specs=(P("space", None), P("tm", None)),
        check_vma=False,
    )
```

time: 241 us -> 129 us (0.54)
  blocking collectives: 198 us -> 0 us
  Pallas kernels: 0 us -> 124 us
  matrix products: 34.5 us -> 0 us
    all_to_all x6 -> x0, blocking collectives: 198 us -> none  [the longest x3 105 us: sent_and_summed(): lax.all_to_all(parts, axis, split_axis=0, concat_axis=0, tiled=True)]
    pallas_call x0 -> x1, Pallas kernels: none -> 124 us  [local(): pl.pallas_call(kernel, name='window', out_shape=[jax.ShapeDtypeStruct((po...]
    dot_general x3 -> x0, matrix products: 34.5 us -> none  [the longest x2 24.9 us: forward(): jnp.dot(block, right, precision=lax.Precision.HIGHEST, preferred_element_...]
where the time goes in v1:
time: 129 us
  Pallas kernels  124 us (96%)
  local copies, waits for them, and re-layouts  4.01 us (3%)
    pallas_call x1, Pallas kernels, local(): pl.pallas_call(kernel, name='window', out_shape=[jax.ShapeDtypeStruct((po...  124 us
    unnamed x2, local copies, waits for them, and re-layouts  4.01 us

profile of v1, /device:TPU:1, one launch (start us, length us, event | category | flops | bytes accessed | tf_op | source)
XLA Modules:
  0.0 129.1 jit_solution(10940359076413682972)
XLA Ops:
  0.6 124.5 %window.1 = (f32[2048,256]{1,0:T(8,128)}, f32[1024,256]{1,0:T(8,128)S(1)}) custom-call(f32[2048,1024]{1,0:T(8,128)} %snap_ref.1, f32[1024,256]{1,0:T(8,128)} %sketch_ref.1), custom_call_target="tpu_custom_call" | custom-call | flops 9663676416 | bytes 8388608 | tf_op jit(solution)/shard_map/window/pallas_call | solution.py:285
  125.1 3.0 %copy.6 = f32[2048,256]{1,0:T(8,128)} copy(f32[2048,256]{1,0:T(8,128)} %get-tuple-element.4) | data formatting | bytes 4194304
  128.1 1.0 copy.7

commit v2 on v1

--- a/solution.py
+++ b/solution.py
@@ -13,6 +13,17 @@
 NZ, NY = 8, 4
 N = 4
 NB = 4
+ORDER_1 = [
+    (0, 0), (0, 1), (1, 0), (0, 2), (1, 1), (0, 3), (2, 0), (1, 2), (1, 3), (2, 1), (3, 0), (2, 2), (2, 3), (3, 1),
+    (4, 0), (3, 2), (3, 3), (4, 1), (5, 0), (4, 2), (4, 3), (6, 0), (5, 1), (6, 1), (5, 2), (5, 3), (6, 2),
+]
+ORDER_B = [
+    (0, 0), (0, 1), (0, 2), (0, 3), (1, 0), (1, 1), (1, 2), (2, 0), (1, 3), (2, 1), (2, 2), (3, 0), (2, 3), (3, 1),
+    (4, 0), (3, 2), (3, 3), (4, 1), (4, 2),
+]
+ORDER_2 = [(stage, i) for stage in range(5) for i in range(N)] + [
+    (5, 0), (5, 1), (6, 0), (5, 2), (6, 1), (5, 3), (6, 2), (6, 3),
+]
 
 
 def split(value):
@@ -201,18 +212,9 @@
 
         return [first, over, finish, spread], arrive, close
 
-    def run(stages, parts, steps):
-        def step(t, _):
-            for s in reversed(range(len(stages))):
-                stage, count = stages[s], parts[s]
-
-                @pl.when((t >= s) & (t < s + count))
-                def _():
-                    stage(t - s)
-
-            return 0
-
-        lax.fori_loop(0, steps, step, 0)
+    def run(stages, order):
+        for stage, part_at in order:
+            stages[stage](part_at)
 
     def multiply_1(i):
         load(i).wait()
@@ -244,7 +246,7 @@
         split_sample(i)
         lax.fori_loop(0, NB, lambda j, _: (add_back(i, j), 0)[1], 0)
 
-    run([*stages, use_sample], [N] * 6 + [N - 1], N + 5)
+    run([*stages, use_sample], ORDER_1)
     arrive_1(N - 1)
     split_sample(N - 1)
 
@@ -265,12 +267,12 @@
         split_cosample(j)
         lax.fori_loop(0, N, lambda i, _: (add_last(i, j), 0)[1], 0)
 
-    run([*stages, use_cosample], [NB] * 4 + [NB - 1], NB + 3)
+    run([*stages, use_cosample], ORDER_B)
     arrive_b(NB - 1)
     split_cosample(NB - 1)
 
     stages, arrive_2, close_2 = tm_stages(1, lambda i: add_last(i, NB - 1), last, refined_ref)
-    run([*stages, arrive_2], [N] * 7, N + 6)
+    run([*stages, arrive_2], ORDER_2)
     close_1()
     close_b()
     close_2()
@@ -286,7 +288,7 @@
         kernel,
         name="window",
         out_shape=[jax.ShapeDtypeStruct((points, k), F32), jax.ShapeDtypeStruct((times, k), F32)],
-        in_specs=[pl.BlockSpec(memory_space=pl.ANY), vmem],
+        in_specs=[pl.BlockSpec(memory_space=pltpu.HBM), vmem],
         out_specs=[vmem, vmem],
         scratch_shapes=[
             pltpu.VMEM((points, times), F32),
@@ -316,7 +318,7 @@
             pltpu.SemaphoreType.DMA((4, NB)),
         ],
         compiler_params=pltpu.CompilerParams(
-            collective_id=0, has_side_effects=True, vmem_limit_bytes=52 << 20
+            collective_id=0, has_side_effects=True, vmem_limit_bytes=40 << 20
         ),
         cost_estimate=pl.CostEstimate(
             flops=18 * points * times * k, bytes_accessed=4 * points * times, transcendentals=0

time: 129 us -> 108 us (0.84)
  Pallas kernels: 124 us -> 101 us
  local copies, waits for them, and re-layouts: 4.01 us -> 6.89 us
    pallas_call x1, Pallas kernels: 124 us -> 101 us  [local(): pl.pallas_call(kernel, name='window', out_shape=[jax.ShapeDtypeStruct((po...]
    unnamed x2 -> x6, local copies, waits for them, and re-layouts: 4.01 us -> 6.89 us
where the time goes in v2:
time: 108 us
  Pallas kernels  101 us (94%)
  local copies, waits for them, and re-layouts  6.89 us (6%)
    pallas_call x1, Pallas kernels, local(): pl.pallas_call(kernel, name='window', out_shape=[jax.ShapeDtypeStruct((po...  101 us
    unnamed x6, local copies, waits for them, and re-layouts  6.89 us

profile of v2, /device:TPU:1, one launch (start us, length us, event | category | flops | bytes accessed | tf_op | source)
XLA Modules:
  0.0 108.3 jit_solution(17500728664175847742)
XLA Ops:
  0.6 0.0 copy-start
  0.6 3.4 %copy-done = f32[2048,1024]{1,0:T(8,128)S(1)} copy-done((f32[2048,1024]{1,0:T(8,128)S(1)}, f32[2048,1024]{1,0:T(8,128)}, u32[]{:S(2)}) %copy-start) | copy-done | bytes 8388632
  4.0 0.0 copy-start.1
  4.0 1.2 %copy-done.1 = f32[1024,256]{1,0:T(8,128)S(1)} copy-done((f32[1024,256]{1,0:T(8,128)S(1)}, f32[1024,256]{1,0:T(8,128)}, u32[]{:S(2)}) %copy-start.1) | copy-done | bytes 1048600
  5.2 100.8 %window.1 = (f32[2048,256]{1,0:T(8,128)S(1)}, f32[1024,256]{1,0:T(8,128)S(1)}) custom-call(f32[2048,1024]{1,0:T(8,128)S(1)} %copy-done, f32[1024,256]{1,0:T(8,128)S(1)} %copy-done.1), custom_call_target="tpu_custom_call" | custom-call | flops 9663676416 | bytes 8388608 | tf_op jit(solution)/shard_map/window/pallas_call | solution.py:287
  106.0 1.3 %copy.6 = f32[2048,256]{1,0:T(8,128)} copy(f32[2048,256]{1,0:T(8,128)S(1)} %get-tuple-element.4) | data formatting | bytes 4194304
  107.3 1.0 copy.7
Async XLA Ops:
  0.6 3.4 %copy-start = (f32[2048,1024]{1,0:T(8,128)S(1)}, f32[2048,1024]{1,0:T(8,128)}, u32[]{:S(2)}) copy-start(f32[2048,1024]{1,0:T(8,128)} %snap_ref.1) | copy-start | bytes 25165828
  4.0 1.2 %copy-start.1 = (f32[1024,256]{1,0:T(8,128)S(1)}, f32[1024,256]{1,0:T(8,128)}, u32[]{:S(2)}) copy-start(f32[1024,256]{1,0:T(8,128)} %sketch_ref.1) | copy-start | bytes 3145732

commit v3 on v0

v3 whole, which is shorter than its diff:
```python
import jax
import jax.numpy as jnp
from jax import lax
from jax.experimental import pallas as pl
from jax.experimental.pallas import tpu as pltpu
from jax.sharding import PartitionSpec as P

EPS = 1e-06
MESH = pl.DeviceIdType.MESH
F32, BF16 = jnp.float32, jnp.bfloat16
NZ, NY = 8, 4
H = 128
N = 4
NB = 4
ORDER = [
    (0, 0, 0, 0), (0, 0, 1, 0), (0, 1, 0, 0), (0, 0, 2, 0), (0, 1, 1, 0), (0, 0, 3, 0), (0, 2, 0, 0), (0, 1, 2, 0),
    (0, 1, 3, 0), (0, 2, 1, 0), (0, 3, 0, 0), (0, 2, 2, 0), (0, 2, 3, 0), (0, 3, 1, 0), (0, 4, 0, 0), (0, 3, 2, 0),
    (0, 3, 3, 0), (0, 3, 0, 1), (0, 3, 1, 1), (0, 4, 1, 0), (0, 3, 2, 1), (0, 3, 3, 1), (0, 5, 0, 0), (0, 4, 2, 0),
    (0, 6, 0, 0), (0, 4, 3, 0), (0, 4, 0, 1), (0, 4, 1, 1), (0, 5, 1, 0), (0, 4, 2, 1), (0, 4, 3, 1), (0, 6, 1, 0),
    (0, 5, 2, 0), (0, 5, 3, 0), (0, 5, 0, 1), (0, 6, 2, 0), (0, 6, 3, 0), (0, 5, 1, 1), (0, 5, 2, 1), (1, 0, 0, 0),
    (1, 0, 1, 0), (0, 5, 3, 1), (1, 0, 2, 0), (1, 0, 3, 0), (0, 6, 0, 1), (0, 6, 1, 1), (0, 6, 2, 1), (0, 6, 3, 1),
    (1, 1, 0, 0), (1, 0, 0, 1), (1, 0, 1, 1), (1, 0, 2, 1), (1, 0, 3, 1), (1, 1, 1, 0), (1, 1, 2, 0), (1, 1, 3, 0),
    (1, 1, 0, 1), (1, 1, 1, 1), (1, 1, 2, 1), (1, 1, 3, 1), (1, 2, 0, 0), (1, 2, 1, 0), (1, 2, 2, 0), (1, 2, 3, 0),
    (1, 2, 0, 1), (1, 2, 1, 1), (1, 2, 2, 1), (1, 2, 3, 1), (1, 3, 0, 0), (1, 3, 1, 0), (1, 3, 2, 0), (1, 4, 0, 0),
    (1, 3, 3, 0), (1, 4, 1, 0), (1, 3, 0, 1), (1, 4, 2, 0), (1, 3, 1, 1), (1, 3, 2, 1), (1, 4, 3, 0), (2, 0, 0, 0),
    (2, 0, 1, 0), (2, 0, 2, 0), (2, 0, 3, 0), (1, 3, 3, 1), (1, 4, 0, 1), (2, 1, 0, 0), (2, 1, 1, 0), (2, 1, 2, 0),
    (2, 1, 3, 0), (1, 4, 1, 1), (1, 4, 2, 1), (1, 4, 3, 1), (2, 2, 0, 0), (2, 0, 0, 1), (2, 0, 1, 1), (2, 2, 1, 0),
    (2, 0, 2, 1), (2, 0, 3, 1), (2, 2, 2, 0), (2, 1, 0, 1), (2, 1, 1, 1), (2, 2, 3, 0), (2, 1, 2, 1), (2, 1, 3, 1),
    (2, 2, 0, 1), (2, 2, 1, 1), (2, 2, 2, 1), (2, 2, 3, 1), (2, 3, 0, 0), (2, 3, 1, 0), (2, 3, 2, 0), (2, 3, 3, 0),
    (2, 4, 0, 0), (2, 4, 1, 0), (2, 4, 2, 0), (2, 4, 3, 0), (2, 5, 0, 0), (2, 5, 1, 0), (2, 6, 0, 0), (2, 5, 2, 0),
    (2, 6, 1, 0), (2, 5, 3, 0), (2, 6, 2, 0), (2, 6, 3, 0),
]


def split(value):
    high = value.astype(BF16)
    return high, (value - high.astype(F32)).astype(BF16)


def scale_halves(left, right):
    squares = jnp.sum(left * left + right * right, axis=1, keepdims=True)
    factor = lax.rsqrt(squares * (1.0 / (2 * H)) + EPS)
    return left * factor, right * factor


def dot(a, b):
    return jnp.dot(a, b, preferred_element_type=F32)


def dot_t(a, b):
    return lax.dot_general(a, b, (((0,), (0,)), ((), ())), preferred_element_type=F32)


def kernel(
    snap_ref, sketch_ref, refined_ref, cosample_ref,
    wide, s_hi, s_lo, b_hi, b_lo, part, sample, p_terms, back, cosample, c_terms, last,
    core_1, y_1, x_1, x2_1, y2_1, core_2, y_2, x_2, x2_2, y2_2, from_xh, from_z,
    load_sem, sent, sum_1, gather_1, got_b, sum_2, gather_2,
):
    points, times = wide.shape
    space, tm = lax.axis_index("space"), lax.axis_index("tm")
    z, xh = space // 2, lax.rem(space, 2)
    xl, y, core = tm // 8, lax.rem(tm // 2, 4), lax.rem(tm, 2)

    def at_tm(xl, y, core):
        return {"space": space, "tm": xl * 8 + y * 2 + core}

    def at_space(z, xh):
        return {"space": z * 2 + xh, "tm": tm}

    other_core, other_x = at_tm(xl, y, 1 - core), at_tm(1 - xl, y, core)
    other_xh = at_space(z, 1 - xh)
    y_at = [lax.rem(y + d, NY) for d in range(NY)]
    z_at = [lax.rem(z + d, NZ) for d in range(NZ)]
    peer_y = [at_tm(xl, y_at[d], core) for d in range(NY)]
    peer_z = [at_space(z_at[d], xh) for d in range(NZ)]
    y_order, z_order = (2, 1, 3), (4, 3, 5, 2, 6, 1, 7)

    chunk, width = points // N, times // NB
    half, sub = chunk // 2, chunk // 4
    half_b = width // 2
    piece = half_b // NZ

    def load(i):
        rows = pl.ds(pl.multiple_of(i * chunk, chunk), chunk)
        return pltpu.make_async_copy(snap_ref.at[rows], wide.at[rows], load_sem.at[i])

    for i in range(N):
        load(i).start()

    barrier = pltpu.get_barrier_semaphore()
    peers = [other_core, other_x, other_xh, *peer_y[1:], *peer_z[1:]]
    for peer in peers:
        pl.semaphore_signal(barrier, inc=1, device_id=peer, device_id_type=MESH)

    b_hi[...], b_lo[...] = split(sketch_ref[...])
    back[...] = jnp.zeros_like(back)
    last[...] = jnp.zeros_like(last)
    pl.semaphore_wait(barrier, len(peers))

    def send(src, dst, sent, arrived, peer):
        pltpu.make_async_remote_copy(
            src_ref=src, dst_ref=dst, send_sem=sent, recv_sem=arrived, device_id=peer, device_id_type=MESH
        ).start()

    def take(rows, columns, sem):
        ref = part.at[pl.ds(0, rows * columns // (2 * H))]
        pltpu.make_async_copy(ref, ref, sem).wait()

    def rows_of(start, size):
        return pl.ds(pl.multiple_of(start, 8), size)

    def mine(i):
        return i * chunk + core * half

    def tm_sums(summed, from_core, from_y, from_x, from_x2, from_y2, sent, got):
        columns = summed.shape[1]

        def first(i):
            src = rows_of(i * chunk + (1 - core) * half, half)
            send(summed.at[src], from_core.at[i], sent.at[0], got.at[0, i], other_core)

        def over_1(i):
            take(half, columns, got.at[0, i])
            a, b = mine(i), mine(i) + sub
            own = rows_of(a, half)
            summed[own, :] += from_core[i]
            for d in y_order:
                src = rows_of(a + y_at[d] * (sub // 4), sub // 4)
                send(summed.at[src], from_y.at[i, d - 1], sent.at[1], got.at[1, i], peer_y[d])
            src = rows_of(b + (1 - xl) * (sub // 2), sub // 2)
            send(summed.at[src], from_x.at[i], sent.at[1], got.at[1, i], other_x)

        def over_2(i):
            take(3 * (sub // 4) + sub // 2, columns, got.at[1, i])
            a, b = mine(i) + y * (sub // 4), mine(i) + sub + xl * (sub // 2)
            own = rows_of(a, sub // 4)
            summed[own, :] += from_y[i, 0] + from_y[i, 1] + from_y[i, 2]
            own = rows_of(b, sub // 2)
            summed[own, :] += from_x[i]
            for d in y_order:
                src = rows_of(b + y_at[d] * (sub // 8), sub // 8)
                send(summed.at[src], from_y2.at[i, d - 1], sent.at[2], got.at[2, i], peer_y[d])
            src = rows_of(a + (1 - xl) * (sub // 8), sub // 8)
            send(summed.at[src], from_x2.at[i], sent.at[2], got.at[2, i], other_x)

        def total(i):
            take(4 * (sub // 8), columns, got.at[2, i])
            a, b = owned(i)
            return (
                summed[a, :] + from_x2[i],
                summed[b, :] + (from_y2[i, 0] + from_y2[i, 1] + from_y2[i, 2]),
            )

        return first, over_1, over_2, total

    def owned(i):
        a = rows_of(mine(i) + y * (sub // 4) + xl * (sub // 8), sub // 8)
        b = rows_of(mine(i) + sub + xl * (sub // 2) + y * (sub // 8), sub // 8)
        return a, b

    def tm_gather(gathered, sent, got):
        columns = gathered.shape[1]

        def move(rows, stage, i, peer):
            send(gathered.at[rows], gathered.at[rows], sent.at[stage], got.at[stage, i], peer)

        def start(i):
            a, b = owned(i)
            for d in y_order:
                move(b, 0, i, peer_y[d])
            move(a, 0, i, other_x)

        def spread(i):
            take(4 * (sub // 8), columns, got.at[0, i])
            a = rows_of(mine(i) + y * (sub // 4), sub // 4)
            b = rows_of(mine(i) + sub + xl * (sub // 2), sub // 2)
            for d in y_order:
                move(a, 1, i, peer_y[d])
            move(b, 1, i, other_x)

        def to_core(i):
            take(3 * (sub // 4) + sub // 2, columns, got.at[1, i])
            move(rows_of(mine(i), half), 2, i, other_core)

        def arrive(i):
            take(half, columns, got.at[2, i])

        return start, spread, to_core, arrive

    def multiply_1(i):
        load(i).wait()

        def step(q, _):
            rows = pl.ds(pl.multiple_of(i * chunk + q * 256, 256), 256)
            high, low = split(wide[rows, :])
            s_hi[rows, :] = high
            s_lo[rows, :] = low
            part[rows, :] = dot(high, b_hi[...]) + (dot(high, b_lo[...]) + dot(low, b_hi[...]))
            return 0

        lax.fori_loop(0, chunk // 256, step, 0)

    def place(i, j):
        rows = pl.ds(pl.multiple_of(i * chunk, chunk), chunk)
        columns = pl.ds(pl.multiple_of(j * width, width), width)
        return rows, columns

    def add_back(i, j, h):
        rows, columns = place(i, j)
        terms = p_terms[h]
        value = dot_t(s_hi[rows, columns], terms) + dot_t(s_lo[rows, columns], terms)
        back[h, columns, :] += value[:, :H] + value[:, H:]

    def add_last(i, j, h):
        rows, columns = place(i, j)
        terms = c_terms[h]
        value = dot(s_hi[rows, columns], terms) + dot(s_lo[rows, columns], terms)
        last[h, rows, :] += value[:, :H] + value[:, H:]

    first_1, over_11, over_12, total_1 = tm_sums(part, core_1, y_1, x_1, x2_1, y2_1, sent.at[0], sum_1)
    gathers_1 = [tm_gather(sample.at[h], sent.at[1], gather_1.at[h]) for h in range(2)]

    def begin_1(i, h):
        multiply_1(i)
        first_1(i)

    def finish_1(i, h):
        if h == 0:
            for rows, value in zip(owned(i), total_1(i)):
                sample[0, rows, :], sample[1, rows, :] = scale_halves(value[:, :H], value[:, H:])
        gathers_1[h][0](i)

    def use_1(i, h):
        gathers_1[h][3](i)
        rows = pl.ds(i * chunk, chunk)
        p_terms[h, :, :H], p_terms[h, :, H:] = split(sample[h, rows, :])
        if i < N - 1:
            lax.fori_loop(0, NB, lambda j, _: (add_back(i, j, h), 0)[1], 0)

    def move_b(rows, stage, j, h, peer):
        send(cosample.at[h, rows], cosample.at[h, rows], sent.at[4, stage], got_b.at[h, stage, j], peer)

    def begin_b(j, h):
        add_back(N - 1, j, h)
        src = rows_of(j * width + (1 - xh) * half_b, half_b)
        send(back.at[h, src], from_xh.at[h, j], sent.at[4, 0], got_b.at[h, 0, j], other_xh)

    def over_b(j, h):
        take(half_b, H, got_b.at[h, 0, j])
        a = j * width + xh * half_b
        own = rows_of(a, half_b)
        back[h, own, :] += from_xh[h, j]
        for d in z_order:
            src = rows_of(a + z_at[d] * piece, piece)
            send(back.at[h, src], from_z.at[h, j, d - 1], sent.at[4, 1], got_b.at[h, 1, j], peer_z[d])

    def finish_b(j, h):
        own = rows_of(j * width + xh * half_b + z * piece, piece)
        if h == 0:
            totals = []
            for g in range(2):
                take(7 * piece, H, got_b.at[g, 1, j])
                total = back[g, own, :]
                for d in range(1, NZ):
                    total += from_z[g, j, d - 1]
                totals.append(total)
            cosample[0, own, :], cosample[1, own, :] = scale_halves(*totals)
        for d in z_order:
            move_b(own, 2, j, h, peer_z[d])

    def spread_b(j, h):
        take(7 * piece, H, got_b.at[h, 2, j])
        move_b(rows_of(j * width + xh * half_b, half_b), 3, j, h, other_xh)

    def use_b(j, h):
        take(half_b, H, got_b.at[h, 3, j])
        rows = pl.ds(j * width, width)
        value = cosample[h, rows, :]
        cosample_ref[rows, h * H : (h + 1) * H] = value
        c_terms[h, :, :H], c_terms[h, :, H:] = split(value)
        if j < NB - 1:
            lax.fori_loop(0, N, lambda i, _: (add_last(i, j, h), 0)[1], 0)

    sums_2 = [
        tm_sums(
            last.at[h], core_2.at[h], y_2.at[h], x_2.at[h], x2_2.at[h], y2_2.at[h], sent.at[2], sum_2.at[h]
        )
        for h in range(2)
    ]
    gather_ends = tm_gather(refined_ref, sent.at[3], gather_2)

    def begin_2(i, h):
        add_last(i, NB - 1, h)
        sums_2[h][0](i)

    def finish_2(i, h):
        left, right = sums_2[0][3](i), sums_2[1][3](i)
        for rows, one, two in zip(owned(i), left, right):
            refined_ref[rows, :H], refined_ref[rows, H:] = scale_halves(one, two)
        gather_ends[0](i)

    stages = [
        [begin_1, lambda i, h: over_11(i), lambda i, h: over_12(i), finish_1]
        + [lambda i, h: gathers_1[h][1](i), lambda i, h: gathers_1[h][2](i), use_1],
        [begin_b, over_b, finish_b, spread_b, use_b],
        [begin_2, lambda i, h: sums_2[h][1](i), lambda i, h: sums_2[h][2](i), finish_2]
        + [lambda i, h: gather_ends[1](i), lambda i, h: gather_ends[2](i), lambda i, h: gather_ends[3](i)],
    ]
    for product, stage, at, h in ORDER:
        stages[product][stage](at, h)

    quarter = 5 * (sub // 4)
    for group, counts in enumerate(
        ([half, quarter, sub // 2], [sub // 2, quarter, half], [half, quarter, sub // 2], [sub // 2, quarter, half])
    ):
        for stage, rows in enumerate(counts):
            take(N * rows, 2 * H, sent.at[group, stage])
    for stage, rows in enumerate((half_b, 7 * piece, 7 * piece, half_b)):
        take(NB * rows, 2 * H, sent.at[4, stage])


def local(snapshots, sketch):
    (points, times), k = snapshots.shape, sketch.shape[1]
    chunk, width = points // N, times // NB
    half, sub, half_b = chunk // 2, chunk // 4, width // 2
    vmem = pl.BlockSpec(memory_space=pltpu.VMEM)
    sums = ((N, half), (N, 3, sub // 4), (N, sub // 2), (N, sub // 8), (N, 3, sub // 8))
    return pl.pallas_call(
        kernel,
        name="window",
        out_shape=[jax.ShapeDtypeStruct((points, k), F32), jax.ShapeDtypeStruct((times, k), F32)],
        in_specs=[pl.BlockSpec(memory_space=pl.ANY), vmem],
        out_specs=[vmem, vmem],
        scratch_shapes=[
            pltpu.VMEM((points, times), F32),
            pltpu.VMEM((points, times), BF16),
            pltpu.VMEM((points, times), BF16),
            pltpu.VMEM((times, k), BF16),
            pltpu.VMEM((times, k), BF16),
            pltpu.VMEM((points, k), F32),
            pltpu.VMEM((2, points, H), F32),
            pltpu.VMEM((2, chunk, 2 * H), BF16),
            pltpu.VMEM((2, times, H), F32),
            pltpu.VMEM((2, times, H), F32),
            pltpu.VMEM((2, width, 2 * H), BF16),
            pltpu.VMEM((2, points, H), F32),
            *[pltpu.VMEM((*shape, k), F32) for shape in sums],
            *[pltpu.VMEM((2, *shape, H), F32) for shape in sums],
            pltpu.VMEM((2, NB, half_b, H), F32),
            pltpu.VMEM((2, NB, NZ - 1, half_b // NZ, H), F32),
            pltpu.SemaphoreType.DMA((N,)),
            pltpu.SemaphoreType.DMA((5, 4)),
            pltpu.SemaphoreType.DMA((3, N)),
            pltpu.SemaphoreType.DMA((2, 3, N)),
            pltpu.SemaphoreType.DMA((2, 4, NB)),
            pltpu.SemaphoreType.DMA((2, 3, N)),
            pltpu.SemaphoreType.DMA((3, N)),
        ],
        compiler_params=pltpu.CompilerParams(
            collective_id=0, has_side_effects=True, vmem_limit_bytes=46 << 20
        ),
        cost_estimate=pl.CostEstimate(
            flops=18 * points * times * k, bytes_accessed=4 * points * times, transcendentals=0
        ),
    )(snapshots, sketch)


def solution(mesh):
    return jax.shard_map(
        local,
        mesh=mesh,
        in_specs=(P("space", "tm"), P("tm", None)),
        out_specs=(P("space", None), P("tm", None)),
        check_vma=False,
    )
```

time: 241 us -> 103 us (0.43)
  blocking collectives: 198 us -> 0 us
  Pallas kernels: 0 us -> 99.2 us
  matrix products: 34.5 us -> 0 us
    all_to_all x6 -> x0, blocking collectives: 198 us -> none  [the longest x3 105 us: sent_and_summed(): lax.all_to_all(parts, axis, split_axis=0, concat_axis=0, tiled=True)]
    pallas_call x0 -> x1, Pallas kernels: none -> 99.2 us  [local(): pl.pallas_call(kernel, name='window', out_shape=[jax.ShapeDtypeStruct((po...]
    dot_general x3 -> x0, matrix products: 34.5 us -> none  [the longest x2 24.9 us: forward(): jnp.dot(block, right, precision=lax.Precision.HIGHEST, preferred_element_...]
where the time goes in v3:
time: 103 us
  Pallas kernels  99.2 us (96%)
  local copies, waits for them, and re-layouts  3.51 us (3%)
    pallas_call x1, Pallas kernels, local(): pl.pallas_call(kernel, name='window', out_shape=[jax.ShapeDtypeStruct((po...  99.2 us
    unnamed x4, local copies, waits for them, and re-layouts  3.51 us

profile of v3, /device:TPU:1, one launch (start us, length us, event | category | flops | bytes accessed | tf_op | source)
XLA Modules:
  0.0 103.3 jit_solution(7962222936983820540)
XLA Ops:
  0.6 0.0 copy-start
  0.6 1.2 %copy-done = f32[1024,256]{1,0:T(8,128)S(1)} copy-done((f32[1024,256]{1,0:T(8,128)S(1)}, f32[1024,256]{1,0:T(8,128)}, u32[]{:S(2)}) %copy-start) | copy-done | bytes 1048600
  1.9 99.2 %window.1 = (f32[2048,256]{1,0:T(8,128)S(1)}, f32[1024,256]{1,0:T(8,128)S(1)}) custom-call(f32[2048,1024]{1,0:T(8,128)} %snap_ref.1, f32[1024,256]{1,0:T(8,128)S(1)} %copy-done), custom_call_target="tpu_custom_call" | custom-call | flops 9663676416 | bytes 8388608 | tf_op jit(solution)/shard_map/window/pallas_call | solution.py:329
  101.1 1.3 %copy.6 = f32[2048,256]{1,0:T(8,128)} copy(f32[2048,256]{1,0:T(8,128)S(1)} %get-tuple-element.4) | data formatting | bytes 4194304
  102.4 1.0 copy.7
Async XLA Ops:
  0.6 1.2 %copy-start = (f32[1024,256]{1,0:T(8,128)S(1)}, f32[1024,256]{1,0:T(8,128)}, u32[]{:S(2)}) copy-start(f32[1024,256]{1,0:T(8,128)} %sketch_ref.1) | copy-start | bytes 3145732

commit v4 on v3

--- a/solution.py
+++ b/solution.py
@@ -12,23 +12,24 @@
 H = 128
 N = 4
 NB = 4
+STEP = 256
 ORDER = [
-    (0, 0, 0, 0), (0, 0, 1, 0), (0, 1, 0, 0), (0, 0, 2, 0), (0, 1, 1, 0), (0, 0, 3, 0), (0, 2, 0, 0), (0, 1, 2, 0),
-    (0, 1, 3, 0), (0, 2, 1, 0), (0, 3, 0, 0), (0, 2, 2, 0), (0, 2, 3, 0), (0, 3, 1, 0), (0, 4, 0, 0), (0, 3, 2, 0),
-    (0, 3, 3, 0), (0, 3, 0, 1), (0, 3, 1, 1), (0, 4, 1, 0), (0, 3, 2, 1), (0, 3, 3, 1), (0, 5, 0, 0), (0, 4, 2, 0),
-    (0, 6, 0, 0), (0, 4, 3, 0), (0, 4, 0, 1), (0, 4, 1, 1), (0, 5, 1, 0), (0, 4, 2, 1), (0, 4, 3, 1), (0, 6, 1, 0),
-    (0, 5, 2, 0), (0, 5, 3, 0), (0, 5, 0, 1), (0, 6, 2, 0), (0, 6, 3, 0), (0, 5, 1, 1), (0, 5, 2, 1), (1, 0, 0, 0),
-    (1, 0, 1, 0), (0, 5, 3, 1), (1, 0, 2, 0), (1, 0, 3, 0), (0, 6, 0, 1), (0, 6, 1, 1), (0, 6, 2, 1), (0, 6, 3, 1),
-    (1, 1, 0, 0), (1, 0, 0, 1), (1, 0, 1, 1), (1, 0, 2, 1), (1, 0, 3, 1), (1, 1, 1, 0), (1, 1, 2, 0), (1, 1, 3, 0),
-    (1, 1, 0, 1), (1, 1, 1, 1), (1, 1, 2, 1), (1, 1, 3, 1), (1, 2, 0, 0), (1, 2, 1, 0), (1, 2, 2, 0), (1, 2, 3, 0),
-    (1, 2, 0, 1), (1, 2, 1, 1), (1, 2, 2, 1), (1, 2, 3, 1), (1, 3, 0, 0), (1, 3, 1, 0), (1, 3, 2, 0), (1, 4, 0, 0),
-    (1, 3, 3, 0), (1, 4, 1, 0), (1, 3, 0, 1), (1, 4, 2, 0), (1, 3, 1, 1), (1, 3, 2, 1), (1, 4, 3, 0), (2, 0, 0, 0),
-    (2, 0, 1, 0), (2, 0, 2, 0), (2, 0, 3, 0), (1, 3, 3, 1), (1, 4, 0, 1), (2, 1, 0, 0), (2, 1, 1, 0), (2, 1, 2, 0),
-    (2, 1, 3, 0), (1, 4, 1, 1), (1, 4, 2, 1), (1, 4, 3, 1), (2, 2, 0, 0), (2, 0, 0, 1), (2, 0, 1, 1), (2, 2, 1, 0),
-    (2, 0, 2, 1), (2, 0, 3, 1), (2, 2, 2, 0), (2, 1, 0, 1), (2, 1, 1, 1), (2, 2, 3, 0), (2, 1, 2, 1), (2, 1, 3, 1),
-    (2, 2, 0, 1), (2, 2, 1, 1), (2, 2, 2, 1), (2, 2, 3, 1), (2, 3, 0, 0), (2, 3, 1, 0), (2, 3, 2, 0), (2, 3, 3, 0),
-    (2, 4, 0, 0), (2, 4, 1, 0), (2, 4, 2, 0), (2, 4, 3, 0), (2, 5, 0, 0), (2, 5, 1, 0), (2, 6, 0, 0), (2, 5, 2, 0),
-    (2, 6, 1, 0), (2, 5, 3, 0), (2, 6, 2, 0), (2, 6, 3, 0),
+    (0, 0, 0, 0), (0, 0, 1, 0), (0, 1, 0, 0), (0, 0, 2, 0), (0, 1, 1, 0), (0, 0, 3, 0), (0, 1, 2, 0), (0, 2, 0, 0),
+    (0, 1, 3, 0), (0, 2, 1, 0), (0, 2, 2, 0), (0, 3, 0, 0), (0, 3, 0, 1), (0, 2, 3, 0), (0, 3, 1, 0), (0, 3, 1, 1),
+    (0, 3, 2, 0), (0, 4, 0, 0), (0, 4, 0, 1), (0, 3, 2, 1), (0, 3, 3, 0), (0, 4, 1, 0), (0, 4, 2, 0), (0, 5, 0, 0),
+    (0, 4, 1, 1), (0, 5, 0, 1), (0, 3, 3, 1), (0, 4, 3, 0), (0, 6, 0, 0), (0, 5, 1, 0), (0, 6, 0, 1), (0, 5, 2, 0),
+    (0, 4, 3, 1), (0, 4, 2, 1), (0, 5, 1, 1), (0, 5, 3, 0), (0, 6, 1, 0), (0, 6, 2, 0), (0, 6, 3, 0), (1, 0, 0, 0),
+    (0, 5, 2, 1), (0, 5, 3, 1), (1, 0, 1, 0), (1, 0, 2, 0), (0, 6, 1, 1), (0, 6, 2, 1), (0, 6, 3, 1), (1, 0, 0, 1),
+    (1, 1, 0, 0), (1, 0, 1, 1), (1, 1, 1, 0), (1, 0, 2, 1), (1, 1, 2, 0), (1, 0, 3, 1), (1, 1, 0, 1), (1, 0, 3, 0),
+    (1, 1, 1, 1), (1, 1, 2, 1), (1, 1, 3, 1), (1, 2, 0, 0), (1, 1, 3, 0), (1, 2, 0, 1), (1, 2, 1, 0), (1, 2, 1, 1),
+    (1, 3, 0, 0), (1, 2, 2, 0), (1, 3, 0, 1), (1, 2, 3, 0), (1, 2, 2, 1), (1, 2, 3, 1), (1, 3, 1, 0), (1, 3, 1, 1),
+    (1, 4, 0, 0), (1, 3, 2, 0), (1, 4, 0, 1), (1, 3, 3, 0), (1, 4, 1, 0), (1, 3, 2, 1), (1, 4, 1, 1), (1, 3, 3, 1),
+    (1, 4, 2, 0), (1, 4, 3, 0), (2, 0, 0, 0), (2, 0, 1, 0), (2, 0, 2, 0), (1, 4, 2, 1), (2, 1, 0, 0), (2, 1, 1, 0),
+    (1, 4, 3, 1), (2, 0, 0, 1), (2, 0, 1, 1), (2, 0, 2, 1), (2, 1, 2, 0), (2, 0, 3, 0), (2, 1, 0, 1), (2, 1, 2, 1),
+    (2, 0, 3, 1), (2, 1, 1, 1), (2, 1, 3, 0), (2, 1, 3, 1), (2, 2, 0, 1), (2, 2, 0, 0), (2, 2, 2, 0), (2, 2, 2, 1),
+    (2, 2, 1, 1), (2, 2, 1, 0), (2, 2, 3, 1), (2, 2, 3, 0), (2, 3, 0, 0), (2, 3, 2, 0), (2, 3, 1, 0), (2, 3, 3, 0),
+    (2, 4, 0, 0), (2, 4, 2, 0), (2, 4, 1, 0), (2, 4, 3, 0), (2, 5, 0, 0), (2, 5, 2, 0), (2, 5, 1, 0), (2, 5, 3, 0),
+    (2, 6, 0, 0), (2, 6, 1, 0), (2, 6, 2, 0), (2, 6, 3, 0),
 ]
 
 
@@ -53,9 +54,9 @@
 
 def kernel(
     snap_ref, sketch_ref, refined_ref, cosample_ref,
-    wide, s_hi, s_lo, b_hi, b_lo, part, sample, p_terms, back, cosample, c_terms, last,
+    wide, sketch, s_hi, s_lo, b_hi, b_lo, part, sample, p_terms, back, cosample, c_terms, last,
     core_1, y_1, x_1, x2_1, y2_1, core_2, y_2, x_2, x2_2, y2_2, from_xh, from_z,
-    load_sem, sent, sum_1, gather_1, got_b, sum_2, gather_2,
+    load_sem, sketch_sem, sent, sum_1, gather_1, got_b, sum_2, gather_2,
 ):
     points, times = wide.shape
     space, tm = lax.axis_index("space"), lax.axis_index("tm")
@@ -81,22 +82,20 @@
     half_b = width // 2
     piece = half_b // NZ
 
-    def load(i):
-        rows = pl.ds(pl.multiple_of(i * chunk, chunk), chunk)
-        return pltpu.make_async_copy(snap_ref.at[rows], wide.at[rows], load_sem.at[i])
-
-    for i in range(N):
-        load(i).start()
+    def load(q):
+        rows = pl.ds(q * STEP, STEP)
+        return pltpu.make_async_copy(snap_ref.at[rows], wide.at[rows], load_sem.at[q])
+
+    load_sketch = pltpu.make_async_copy(sketch_ref, sketch, sketch_sem)
+    load_sketch.start()
+    for q in range(points // STEP):
+        load(q).start()
 
     barrier = pltpu.get_barrier_semaphore()
     peers = [other_core, other_x, other_xh, *peer_y[1:], *peer_z[1:]]
     for peer in peers:
         pl.semaphore_signal(barrier, inc=1, device_id=peer, device_id_type=MESH)
 
-    b_hi[...], b_lo[...] = split(sketch_ref[...])
-    back[...] = jnp.zeros_like(back)
-    last[...] = jnp.zeros_like(last)
-    pl.semaphore_wait(barrier, len(peers))
 
     def send(src, dst, sent, arrived, peer):
         pltpu.make_async_remote_copy(
@@ -189,40 +188,40 @@
         return start, spread, to_core, arrive
 
     def multiply_1(i):
-        load(i).wait()
-
-        def step(q, _):
-            rows = pl.ds(pl.multiple_of(i * chunk + q * 256, 256), 256)
+        size = STEP if i == 0 else chunk
+        for start in range(i * chunk, (i + 1) * chunk, size):
+            for q in range(start // STEP, (start + size) // STEP):
+                load(q).wait()
+            rows = pl.ds(start, size)
             high, low = split(wide[rows, :])
             s_hi[rows, :] = high
             s_lo[rows, :] = low
             part[rows, :] = dot(high, b_hi[...]) + (dot(high, b_lo[...]) + dot(low, b_hi[...]))
-            return 0
-
-        lax.fori_loop(0, chunk // 256, step, 0)
-
-    def place(i, j):
-        rows = pl.ds(pl.multiple_of(i * chunk, chunk), chunk)
-        columns = pl.ds(pl.multiple_of(j * width, width), width)
-        return rows, columns
-
-    def add_back(i, j, h):
-        rows, columns = place(i, j)
+
+    def add_back(i, h):
+        rows = pl.ds(i * chunk, chunk)
         terms = p_terms[h]
-        value = dot_t(s_hi[rows, columns], terms) + dot_t(s_lo[rows, columns], terms)
-        back[h, columns, :] += value[:, :H] + value[:, H:]
-
-    def add_last(i, j, h):
-        rows, columns = place(i, j)
+        value = dot_t(s_hi[rows, :], terms) + dot_t(s_lo[rows, :], terms)
+        value = value[:, :H] + value[:, H:]
+        back[h] = value if i == 0 else back[h] + value
+
+    def add_last(rows, j, h):
+        columns = pl.ds(j * width, width)
         terms = c_terms[h]
         value = dot(s_hi[rows, columns], terms) + dot(s_lo[rows, columns], terms)
-        last[h, rows, :] += value[:, :H] + value[:, H:]
+        value = value[:, :H] + value[:, H:]
+        last[h, rows, :] = value if j == 0 else last[h, rows, :] + value
 
     first_1, over_11, over_12, total_1 = tm_sums(part, core_1, y_1, x_1, x2_1, y2_1, sent.at[0], sum_1)
     gathers_1 = [tm_gather(sample.at[h], sent.at[1], gather_1.at[h]) for h in range(2)]
 
     def begin_1(i, h):
+        if i == 0:
+            load_sketch.wait()
+            b_hi[...], b_lo[...] = split(sketch[...])
         multiply_1(i)
+        if i == 0:
+            pl.semaphore_wait(barrier, len(peers))
         first_1(i)
 
     def finish_1(i, h):
@@ -236,13 +235,14 @@
         rows = pl.ds(i * chunk, chunk)
         p_terms[h, :, :H], p_terms[h, :, H:] = split(sample[h, rows, :])
         if i < N - 1:
-            lax.fori_loop(0, NB, lambda j, _: (add_back(i, j, h), 0)[1], 0)
+            add_back(i, h)
 
     def move_b(rows, stage, j, h, peer):
         send(cosample.at[h, rows], cosample.at[h, rows], sent.at[4, stage], got_b.at[h, stage, j], peer)
 
     def begin_b(j, h):
-        add_back(N - 1, j, h)
+        if j == 0:
+            add_back(N - 1, h)
         src = rows_of(j * width + (1 - xh) * half_b, half_b)
         send(back.at[h, src], from_xh.at[h, j], sent.at[4, 0], got_b.at[h, 0, j], other_xh)
 
@@ -280,7 +280,7 @@
         cosample_ref[rows, h * H : (h + 1) * H] = value
         c_terms[h, :, :H], c_terms[h, :, H:] = split(value)
         if j < NB - 1:
-            lax.fori_loop(0, N, lambda i, _: (add_last(i, j, h), 0)[1], 0)
+            add_last(pl.ds(0, points), j, h)
 
     sums_2 = [
         tm_sums(
@@ -291,7 +291,8 @@
     gather_ends = tm_gather(refined_ref, sent.at[3], gather_2)
 
     def begin_2(i, h):
-        add_last(i, NB - 1, h)
+        if i % (N // 2) == 0:
+            add_last(pl.ds(i * chunk, points // 2), NB - 1, h)
         sums_2[h][0](i)
 
     def finish_2(i, h):
@@ -330,10 +331,11 @@
         kernel,
         name="window",
         out_shape=[jax.ShapeDtypeStruct((points, k), F32), jax.ShapeDtypeStruct((times, k), F32)],
-        in_specs=[pl.BlockSpec(memory_space=pl.ANY), vmem],
+        in_specs=[pl.BlockSpec(memory_space=pl.ANY)] * 2,
         out_specs=[vmem, vmem],
         scratch_shapes=[
             pltpu.VMEM((points, times), F32),
+            pltpu.VMEM((times, k), F32),
             pltpu.VMEM((points, times), BF16),
             pltpu.VMEM((points, times), BF16),
             pltpu.VMEM((times, k), BF16),
@@ -349,7 +351,8 @@
             *[pltpu.VMEM((2, *shape, H), F32) for shape in sums],
             pltpu.VMEM((2, NB, half_b, H), F32),
             pltpu.VMEM((2, NB, NZ - 1, half_b // NZ, H), F32),
-            pltpu.SemaphoreType.DMA((N,)),
+            pltpu.SemaphoreType.DMA((points // STEP,)),
+            pltpu.SemaphoreType.DMA,
             pltpu.SemaphoreType.DMA((5, 4)),
             pltpu.SemaphoreType.DMA((3, N)),
             pltpu.SemaphoreType.DMA((2, 3, N)),

time: 103 us -> 99.7 us (0.968)
  Pallas kernels: 99.2 us -> 95.5 us
    pallas_call x1, Pallas kernels: 99.2 us -> 95.5 us  [local(): pl.pallas_call(kernel, name='window', out_shape=[jax.ShapeDtypeStruct((po...]
where the time goes in v4:
time: 99.7 us; the launch traced here: 99.6 us
  Pallas kernels  95.5 us (96%)
  local copies, waits for them, and re-layouts  3.51 us (4%)
    pallas_call x1, Pallas kernels, local(): pl.pallas_call(kernel, name='window', out_shape=[jax.ShapeDtypeStruct((po...  95.5 us
    unnamed x4, local copies, waits for them, and re-layouts  3.51 us

profile of v4, /device:TPU:1, one launch (start us, length us, event | category | flops | bytes accessed | tf_op | source)
XLA Modules:
  0.0 99.6 jit_solution(5542829673333534779)
XLA Ops:
  0.6 0.0 copy-start
  0.6 1.2 %copy-done = f32[1024,256]{1,0:T(8,128)S(1)} copy-done((f32[1024,256]{1,0:T(8,128)S(1)}, f32[1024,256]{1,0:T(8,128)}, u32[]{:S(2)}) %copy-start) | copy-done | bytes 1048600
  1.9 95.5 %window.1 = (f32[2048,256]{1,0:T(8,128)S(1)}, f32[1024,256]{1,0:T(8,128)S(1)}) custom-call(f32[2048,1024]{1,0:T(8,128)} %snap_ref.1, f32[1024,256]{1,0:T(8,128)S(1)} %copy-done), custom_call_target="tpu_custom_call" | custom-call | flops 9663676416 | bytes 8388608 | tf_op jit(solution)/shard_map/window/pallas_call | solution.py:330
  97.3 1.3 %copy.6 = f32[2048,256]{1,0:T(8,128)} copy(f32[2048,256]{1,0:T(8,128)S(1)} %get-tuple-element.4) | data formatting | bytes 4194304
  98.6 1.0 copy.7
Async XLA Ops:
  0.6 1.2 %copy-start = (f32[1024,256]{1,0:T(8,128)S(1)}, f32[1024,256]{1,0:T(8,128)}, u32[]{:S(2)}) copy-start(f32[1024,256]{1,0:T(8,128)} %sketch_ref.1) | copy-start | bytes 3145732

commit v5 on v4

--- a/solution.py
+++ b/solution.py
@@ -14,22 +14,35 @@
 NB = 4
 STEP = 256
 ORDER = [
-    (0, 0, 0, 0), (0, 0, 1, 0), (0, 1, 0, 0), (0, 0, 2, 0), (0, 1, 1, 0), (0, 0, 3, 0), (0, 1, 2, 0), (0, 2, 0, 0),
-    (0, 1, 3, 0), (0, 2, 1, 0), (0, 2, 2, 0), (0, 3, 0, 0), (0, 3, 0, 1), (0, 2, 3, 0), (0, 3, 1, 0), (0, 3, 1, 1),
-    (0, 3, 2, 0), (0, 4, 0, 0), (0, 4, 0, 1), (0, 3, 2, 1), (0, 3, 3, 0), (0, 4, 1, 0), (0, 4, 2, 0), (0, 5, 0, 0),
-    (0, 4, 1, 1), (0, 5, 0, 1), (0, 3, 3, 1), (0, 4, 3, 0), (0, 6, 0, 0), (0, 5, 1, 0), (0, 6, 0, 1), (0, 5, 2, 0),
-    (0, 4, 3, 1), (0, 4, 2, 1), (0, 5, 1, 1), (0, 5, 3, 0), (0, 6, 1, 0), (0, 6, 2, 0), (0, 6, 3, 0), (1, 0, 0, 0),
-    (0, 5, 2, 1), (0, 5, 3, 1), (1, 0, 1, 0), (1, 0, 2, 0), (0, 6, 1, 1), (0, 6, 2, 1), (0, 6, 3, 1), (1, 0, 0, 1),
-    (1, 1, 0, 0), (1, 0, 1, 1), (1, 1, 1, 0), (1, 0, 2, 1), (1, 1, 2, 0), (1, 0, 3, 1), (1, 1, 0, 1), (1, 0, 3, 0),
-    (1, 1, 1, 1), (1, 1, 2, 1), (1, 1, 3, 1), (1, 2, 0, 0), (1, 1, 3, 0), (1, 2, 0, 1), (1, 2, 1, 0), (1, 2, 1, 1),
-    (1, 3, 0, 0), (1, 2, 2, 0), (1, 3, 0, 1), (1, 2, 3, 0), (1, 2, 2, 1), (1, 2, 3, 1), (1, 3, 1, 0), (1, 3, 1, 1),
-    (1, 4, 0, 0), (1, 3, 2, 0), (1, 4, 0, 1), (1, 3, 3, 0), (1, 4, 1, 0), (1, 3, 2, 1), (1, 4, 1, 1), (1, 3, 3, 1),
-    (1, 4, 2, 0), (1, 4, 3, 0), (2, 0, 0, 0), (2, 0, 1, 0), (2, 0, 2, 0), (1, 4, 2, 1), (2, 1, 0, 0), (2, 1, 1, 0),
-    (1, 4, 3, 1), (2, 0, 0, 1), (2, 0, 1, 1), (2, 0, 2, 1), (2, 1, 2, 0), (2, 0, 3, 0), (2, 1, 0, 1), (2, 1, 2, 1),
-    (2, 0, 3, 1), (2, 1, 1, 1), (2, 1, 3, 0), (2, 1, 3, 1), (2, 2, 0, 1), (2, 2, 0, 0), (2, 2, 2, 0), (2, 2, 2, 1),
-    (2, 2, 1, 1), (2, 2, 1, 0), (2, 2, 3, 1), (2, 2, 3, 0), (2, 3, 0, 0), (2, 3, 2, 0), (2, 3, 1, 0), (2, 3, 3, 0),
-    (2, 4, 0, 0), (2, 4, 2, 0), (2, 4, 1, 0), (2, 4, 3, 0), (2, 5, 0, 0), (2, 5, 2, 0), (2, 5, 1, 0), (2, 5, 3, 0),
-    (2, 6, 0, 0), (2, 6, 1, 0), (2, 6, 2, 0), (2, 6, 3, 0),
+    (0, 0, 0, 0, 0), (0, 0, 1, 0, 0), (0, 1, 0, 0, 0), (0, 0, 2, 0, 0), (0, 1, 1, 0, 0), (0, 0, 3, 0, 0),
+    (0, 1, 2, 0, 0), (0, 2, 0, 0, 1), (0, 2, 0, 0, 0), (0, 1, 3, 0, 0), (0, 2, 1, 0, 0), (0, 2, 1, 0, 1),
+    (0, 3, 0, 0, 0), (0, 2, 2, 0, 1), (0, 3, 0, 1, 0), (0, 2, 2, 0, 0), (0, 3, 0, 0, 1), (0, 3, 0, 1, 1),
+    (0, 2, 3, 0, 1), (0, 2, 3, 0, 0), (0, 4, 0, 0, 0), (0, 3, 1, 0, 0), (0, 3, 1, 0, 1), (0, 4, 0, 1, 0),
+    (0, 3, 2, 0, 0), (0, 3, 2, 1, 0), (0, 3, 1, 1, 0), (0, 3, 2, 0, 1), (0, 4, 0, 0, 1), (0, 3, 1, 1, 1),
+    (0, 3, 3, 0, 0), (0, 3, 2, 1, 1), (0, 4, 0, 1, 1), (0, 3, 3, 0, 1), (0, 4, 1, 0, 0), (0, 4, 2, 0, 0),
+    (0, 3, 3, 1, 1), (0, 5, 0, 0, 0), (0, 4, 1, 1, 0), (0, 4, 1, 0, 1), (0, 5, 0, 0, 1), (0, 4, 3, 0, 0),
+    (0, 4, 2, 1, 0), (0, 5, 0, 1, 0), (0, 4, 2, 0, 1), (0, 3, 3, 1, 0), (0, 5, 0, 1, 1), (0, 4, 2, 1, 1),
+    (0, 6, 0, 0, 0), (0, 4, 3, 0, 1), (0, 5, 1, 0, 0), (0, 4, 1, 1, 1), (0, 5, 1, 0, 1), (0, 6, 0, 1, 0),
+    (0, 5, 2, 0, 1), (0, 5, 2, 0, 0), (0, 4, 3, 1, 0), (0, 6, 1, 0, 0), (0, 5, 3, 0, 0), (0, 5, 3, 0, 1),
+    (0, 4, 3, 1, 1), (0, 5, 1, 1, 0), (0, 6, 2, 0, 0), (0, 5, 1, 1, 1), (0, 6, 3, 0, 0), (1, 0, 0, 0, 0),
+    (0, 5, 2, 1, 1), (0, 5, 2, 1, 0), (1, 0, 1, 0, 0), (0, 5, 3, 1, 1), (0, 6, 1, 1, 0), (0, 5, 3, 1, 0),
+    (0, 6, 2, 1, 0), (1, 0, 2, 0, 0), (0, 6, 3, 1, 0), (1, 0, 0, 1, 0), (1, 1, 0, 0, 0), (1, 0, 1, 1, 0),
+    (1, 1, 1, 0, 0), (1, 0, 2, 1, 0), (1, 0, 3, 0, 0), (1, 1, 2, 0, 0), (1, 0, 3, 1, 0), (1, 1, 0, 1, 0),
+    (1, 1, 1, 1, 0), (1, 1, 2, 1, 0), (1, 1, 3, 0, 0), (1, 2, 0, 0, 0), (1, 1, 3, 1, 0), (1, 2, 1, 0, 0),
+    (1, 2, 2, 0, 0), (1, 2, 0, 1, 0), (1, 3, 0, 0, 0), (1, 2, 3, 0, 0), (1, 2, 1, 1, 0), (1, 2, 2, 1, 0),
+    (1, 3, 1, 0, 0), (1, 3, 2, 0, 0), (1, 4, 0, 0, 0), (1, 3, 0, 1, 0), (1, 2, 3, 1, 0), (1, 3, 3, 0, 0),
+    (1, 4, 1, 0, 0), (1, 3, 1, 1, 0), (1, 4, 2, 0, 0), (1, 3, 2, 1, 0), (1, 4, 0, 1, 0), (1, 4, 3, 0, 0),
+    (1, 3, 3, 1, 0), (2, 0, 0, 0, 0), (2, 0, 1, 0, 0), (2, 0, 2, 0, 0), (2, 0, 3, 0, 0), (1, 4, 1, 1, 0),
+    (2, 1, 0, 0, 0), (1, 4, 2, 1, 0), (2, 1, 3, 0, 0), (2, 1, 1, 0, 0), (1, 4, 3, 1, 0), (2, 0, 0, 1, 0),
+    (2, 1, 2, 0, 0), (2, 0, 1, 1, 0), (2, 0, 2, 1, 0), (2, 2, 0, 0, 1), (2, 0, 3, 1, 0), (2, 1, 0, 1, 0),
+    (2, 1, 1, 1, 0), (2, 1, 2, 1, 0), (2, 1, 3, 1, 0), (2, 2, 0, 1, 1), (2, 2, 1, 0, 1), (2, 2, 1, 0, 0),
+    (2, 2, 0, 0, 0), (2, 2, 0, 1, 0), (2, 2, 1, 1, 1), (2, 2, 2, 0, 1), (2, 2, 2, 1, 1), (2, 2, 2, 0, 0),
+    (2, 2, 3, 0, 1), (2, 2, 1, 1, 0), (2, 2, 2, 1, 0), (2, 2, 3, 1, 1), (2, 2, 3, 0, 0), (2, 2, 3, 1, 0),
+    (2, 3, 0, 0, 1), (2, 3, 0, 0, 0), (2, 3, 1, 0, 1), (2, 3, 1, 0, 0), (2, 3, 2, 0, 1), (2, 3, 3, 0, 0),
+    (2, 3, 3, 0, 1), (2, 3, 2, 0, 0), (2, 4, 0, 0, 0), (2, 4, 0, 0, 1), (2, 4, 1, 0, 0), (2, 4, 3, 0, 0),
+    (2, 4, 2, 0, 1), (2, 4, 2, 0, 0), (2, 4, 3, 0, 1), (2, 4, 1, 0, 1), (2, 5, 0, 0, 0), (2, 5, 3, 0, 1),
+    (2, 5, 1, 0, 0), (2, 5, 3, 0, 0), (2, 5, 2, 0, 1), (2, 5, 0, 0, 1), (2, 5, 1, 0, 1), (2, 5, 2, 0, 0),
+    (2, 6, 3, 0, 0), (2, 6, 0, 0, 0), (2, 6, 1, 0, 0), (2, 6, 2, 0, 0),
 ]
 
 
@@ -128,62 +141,73 @@
                 src = rows_of(a + y_at[d] * (sub // 4), sub // 4)
                 send(summed.at[src], from_y.at[i, d - 1], sent.at[1], got.at[1, i], peer_y[d])
             src = rows_of(b + (1 - xl) * (sub // 2), sub // 2)
-            send(summed.at[src], from_x.at[i], sent.at[1], got.at[1, i], other_x)
-
-        def over_2(i):
-            take(3 * (sub // 4) + sub // 2, columns, got.at[1, i])
-            a, b = mine(i) + y * (sub // 4), mine(i) + sub + xl * (sub // 2)
-            own = rows_of(a, sub // 4)
-            summed[own, :] += from_y[i, 0] + from_y[i, 1] + from_y[i, 2]
-            own = rows_of(b, sub // 2)
-            summed[own, :] += from_x[i]
-            for d in y_order:
-                src = rows_of(b + y_at[d] * (sub // 8), sub // 8)
-                send(summed.at[src], from_y2.at[i, d - 1], sent.at[2], got.at[2, i], peer_y[d])
-            src = rows_of(a + (1 - xl) * (sub // 8), sub // 8)
-            send(summed.at[src], from_x2.at[i], sent.at[2], got.at[2, i], other_x)
-
-        def total(i):
-            take(4 * (sub // 8), columns, got.at[2, i])
-            a, b = owned(i)
-            return (
-                summed[a, :] + from_x2[i],
-                summed[b, :] + (from_y2[i, 0] + from_y2[i, 1] + from_y2[i, 2]),
-            )
+            send(summed.at[src], from_x.at[i], sent.at[1], got.at[2, i], other_x)
+
+        def over_2(i, p):
+            if p == 0:
+                take(3 * (sub // 4), columns, got.at[1, i])
+                a = mine(i) + y * (sub // 4)
+                own = rows_of(a, sub // 4)
+                summed[own, :] += from_y[i, 0] + from_y[i, 1] + from_y[i, 2]
+                src = rows_of(a + (1 - xl) * (sub // 8), sub // 8)
+                send(summed.at[src], from_x2.at[i], sent.at[2], got.at[3, i], other_x)
+            else:
+                take(sub // 2, columns, got.at[2, i])
+                b = mine(i) + sub + xl * (sub // 2)
+                own = rows_of(b, sub // 2)
+                summed[own, :] += from_x[i]
+                for d in y_order:
+                    src = rows_of(b + y_at[d] * (sub // 8), sub // 8)
+                    send(summed.at[src], from_y2.at[i, d - 1], sent.at[2], got.at[4, i], peer_y[d])
+
+        def total(i, p):
+            own = owned(i, p)
+            if p == 0:
+                take(sub // 8, columns, got.at[3, i])
+                return summed[own, :] + from_x2[i]
+            take(3 * (sub // 8), columns, got.at[4, i])
+            return summed[own, :] + (from_y2[i, 0] + from_y2[i, 1] + from_y2[i, 2])
 
         return first, over_1, over_2, total
 
-    def owned(i):
-        a = rows_of(mine(i) + y * (sub // 4) + xl * (sub // 8), sub // 8)
-        b = rows_of(mine(i) + sub + xl * (sub // 2) + y * (sub // 8), sub // 8)
-        return a, b
+    def owned(i, p):
+        if p == 0:
+            return rows_of(mine(i) + y * (sub // 4) + xl * (sub // 8), sub // 8)
+        return rows_of(mine(i) + sub + xl * (sub // 2) + y * (sub // 8), sub // 8)
 
     def tm_gather(gathered, sent, got):
         columns = gathered.shape[1]
 
-        def move(rows, stage, i, peer):
-            send(gathered.at[rows], gathered.at[rows], sent.at[stage], got.at[stage, i], peer)
-
-        def start(i):
-            a, b = owned(i)
-            for d in y_order:
-                move(b, 0, i, peer_y[d])
-            move(a, 0, i, other_x)
-
-        def spread(i):
-            take(4 * (sub // 8), columns, got.at[0, i])
-            a = rows_of(mine(i) + y * (sub // 4), sub // 4)
-            b = rows_of(mine(i) + sub + xl * (sub // 2), sub // 2)
-            for d in y_order:
-                move(a, 1, i, peer_y[d])
-            move(b, 1, i, other_x)
-
-        def to_core(i):
-            take(3 * (sub // 4) + sub // 2, columns, got.at[1, i])
-            move(rows_of(mine(i), half), 2, i, other_core)
+        def move(rows, stage, place, i, peer):
+            send(gathered.at[rows], gathered.at[rows], sent.at[stage], got.at[place, i], peer)
+
+        def start(i, p):
+            own = owned(i, p)
+            if p == 0:
+                move(own, 0, 0, i, other_x)
+            else:
+                for d in y_order:
+                    move(own, 0, 1, i, peer_y[d])
+
+        def spread(i, p):
+            if p == 0:
+                take(sub // 8, columns, got.at[0, i])
+                rows = rows_of(mine(i) + y * (sub // 4), sub // 4)
+                for d in y_order:
+                    move(rows, 1, 2, i, peer_y[d])
+            else:
+                take(3 * (sub // 8), columns, got.at[1, i])
+                move(rows_of(mine(i) + sub + xl * (sub // 2), sub // 2), 1, 3, i, other_x)
+
+        def to_core(i, p):
+            if p == 0:
+                take(3 * (sub // 4), columns, got.at[2, i])
+            else:
+                take(sub // 2, columns, got.at[3, i])
+            move(rows_of(mine(i) + p * sub, sub), 2, 4, i, other_core)
 
         def arrive(i):
-            take(half, columns, got.at[2, i])
+            take(half, columns, got.at[4, i])
 
         return start, spread, to_core, arrive
 
@@ -215,7 +239,7 @@
     first_1, over_11, over_12, total_1 = tm_sums(part, core_1, y_1, x_1, x2_1, y2_1, sent.at[0], sum_1)
     gathers_1 = [tm_gather(sample.at[h], sent.at[1], gather_1.at[h]) for h in range(2)]
 
-    def begin_1(i, h):
+    def begin_1(i, h, p):
         if i == 0:
             load_sketch.wait()
             b_hi[...], b_lo[...] = split(sketch[...])
@@ -224,13 +248,13 @@
             pl.semaphore_wait(barrier, len(peers))
         first_1(i)
 
-    def finish_1(i, h):
+    def finish_1(i, h, p):
         if h == 0:
-            for rows, value in zip(owned(i), total_1(i)):
-                sample[0, rows, :], sample[1, rows, :] = scale_halves(value[:, :H], value[:, H:])
-        gathers_1[h][0](i)
-
-    def use_1(i, h):
+            rows, value = owned(i, p), total_1(i, p)
+            sample[0, rows, :], sample[1, rows, :] = scale_halves(value[:, :H], value[:, H:])
+        gathers_1[h][0](i, p)
+
+    def use_1(i, h, p):
         gathers_1[h][3](i)
         rows = pl.ds(i * chunk, chunk)
         p_terms[h, :, :H], p_terms[h, :, H:] = split(sample[h, rows, :])
@@ -240,13 +264,13 @@
     def move_b(rows, stage, j, h, peer):
         send(cosample.at[h, rows], cosample.at[h, rows], sent.at[4, stage], got_b.at[h, stage, j], peer)
 
-    def begin_b(j, h):
+    def begin_b(j, h, p):
         if j == 0:
             add_back(N - 1, h)
         src = rows_of(j * width + (1 - xh) * half_b, half_b)
         send(back.at[h, src], from_xh.at[h, j], sent.at[4, 0], got_b.at[h, 0, j], other_xh)
 
-    def over_b(j, h):
+    def over_b(j, h, p):
         take(half_b, H, got_b.at[h, 0, j])
         a = j * width + xh * half_b
         own = rows_of(a, half_b)
@@ -255,7 +279,7 @@
             src = rows_of(a + z_at[d] * piece, piece)
             send(back.at[h, src], from_z.at[h, j, d - 1], sent.at[4, 1], got_b.at[h, 1, j], peer_z[d])
 
-    def finish_b(j, h):
+    def finish_b(j, h, p):
         own = rows_of(j * width + xh * half_b + z * piece, piece)
         if h == 0:
             totals = []
@@ -269,11 +293,11 @@
         for d in z_order:
             move_b(own, 2, j, h, peer_z[d])
 
-    def spread_b(j, h):
+    def spread_b(j, h, p):
         take(7 * piece, H, got_b.at[h, 2, j])
         move_b(rows_of(j * width + xh * half_b, half_b), 3, j, h, other_xh)
 
-    def use_b(j, h):
+    def use_b(j, h, p):
         take(half_b, H, got_b.at[h, 3, j])
         rows = pl.ds(j * width, width)
         value = cosample[h, rows, :]
@@ -290,26 +314,26 @@
     ]
     gather_ends = tm_gather(refined_ref, sent.at[3], gather_2)
 
-    def begin_2(i, h):
+    def begin_2(i, h, p):
         if i % (N // 2) == 0:
             add_last(pl.ds(i * chunk, points // 2), NB - 1, h)
         sums_2[h][0](i)
 
-    def finish_2(i, h):
-        left, right = sums_2[0][3](i), sums_2[1][3](i)
-        for rows, one, two in zip(owned(i), left, right):
-            refined_ref[rows, :H], refined_ref[rows, H:] = scale_halves(one, two)
-        gather_ends[0](i)
+    def finish_2(i, h, p):
+        rows = owned(i, p)
+        refined_ref[rows, :H], refined_ref[rows, H:] = scale_halves(sums_2[0][3](i, p), sums_2[1][3](i, p))
+        gather_ends[0](i, p)
 
     stages = [
-        [begin_1, lambda i, h: over_11(i), lambda i, h: over_12(i), finish_1]
-        + [lambda i, h: gathers_1[h][1](i), lambda i, h: gathers_1[h][2](i), use_1],
+        [begin_1, lambda i, h, p: over_11(i), lambda i, h, p: over_12(i, p), finish_1]
+        + [lambda i, h, p: gathers_1[h][1](i, p), lambda i, h, p: gathers_1[h][2](i, p), use_1],
         [begin_b, over_b, finish_b, spread_b, use_b],
-        [begin_2, lambda i, h: sums_2[h][1](i), lambda i, h: sums_2[h][2](i), finish_2]
-        + [lambda i, h: gather_ends[1](i), lambda i, h: gather_ends[2](i), lambda i, h: gather_ends[3](i)],
+        [begin_2, lambda i, h, p: sums_2[h][1](i), lambda i, h, p: sums_2[h][2](i, p), finish_2]
+        + [lambda i, h, p: gather_ends[1](i, p), lambda i, h, p: gather_ends[2](i, p)]
+        + [lambda i, h, p: gather_ends[3](i)],
     ]
-    for product, stage, at, h in ORDER:
-        stages[product][stage](at, h)
+    for product, stage, at, h, p in ORDER:
+        stages[product][stage](at, h, p)
 
     quarter = 5 * (sub // 4)
     for group, counts in enumerate(
@@ -354,11 +378,11 @@
             pltpu.SemaphoreType.DMA((points // STEP,)),
             pltpu.SemaphoreType.DMA,
             pltpu.SemaphoreType.DMA((5, 4)),
-            pltpu.SemaphoreType.DMA((3, N)),
-            pltpu.SemaphoreType.DMA((2, 3, N)),
+            pltpu.SemaphoreType.DMA((5, N)),
+            pltpu.SemaphoreType.DMA((2, 5, N)),
             pltpu.SemaphoreType.DMA((2, 4, NB)),
-            pltpu.SemaphoreType.DMA((2, 3, N)),
-            pltpu.SemaphoreType.DMA((3, N)),
+            pltpu.SemaphoreType.DMA((2, 5, N)),
+            pltpu.SemaphoreType.DMA((5, N)),
         ],
         compiler_params=pltpu.CompilerParams(
             collective_id=0, has_side_effects=True, vmem_limit_bytes=46 << 20

time: 99.7 us -> 98.3 us (0.986)
  Pallas kernels: 95.5 us -> 94.1 us
    pallas_call x1, Pallas kernels: 95.5 us -> 94.1 us  [local(): pl.pallas_call(kernel, name='window', out_shape=[jax.ShapeDtypeStruct((po...]
where the time goes in v5:
time: 98.3 us; the launch traced here: 98.2 us
  Pallas kernels  94.1 us (96%)
  local copies, waits for them, and re-layouts  3.51 us (4%)
    pallas_call x1, Pallas kernels, local(): pl.pallas_call(kernel, name='window', out_shape=[jax.ShapeDtypeStruct((po...  94.1 us
    unnamed x4, local copies, waits for them, and re-layouts  3.51 us

profile of v5, /device:TPU:1, one launch (start us, length us, event | category | flops | bytes accessed | tf_op | source)
XLA Modules:
  0.0 98.2 jit_solution(9888024754813777248)
XLA Ops:
  0.6 0.0 copy-start
  0.6 1.2 %copy-done = f32[1024,256]{1,0:T(8,128)S(1)} copy-done((f32[1024,256]{1,0:T(8,128)S(1)}, f32[1024,256]{1,0:T(8,128)}, u32[]{:S(2)}) %copy-start) | copy-done | bytes 1048600
  1.9 94.1 %window.1 = (f32[2048,256]{1,0:T(8,128)S(1)}, f32[1024,256]{1,0:T(8,128)S(1)}) custom-call(f32[2048,1024]{1,0:T(8,128)} %snap_ref.1, f32[1024,256]{1,0:T(8,128)S(1)} %copy-done), custom_call_target="tpu_custom_call" | custom-call | flops 9663676416 | bytes 8388608 | tf_op jit(solution)/shard_map/window/pallas_call | solution.py:354
  95.9 1.3 %copy.6 = f32[2048,256]{1,0:T(8,128)} copy(f32[2048,256]{1,0:T(8,128)S(1)} %get-tuple-element.4) | data formatting | bytes 4194304
  97.2 1.0 copy.7
Async XLA Ops:
  0.6 1.2 %copy-start = (f32[1024,256]{1,0:T(8,128)S(1)}, f32[1024,256]{1,0:T(8,128)}, u32[]{:S(2)}) copy-start(f32[1024,256]{1,0:T(8,128)} %sketch_ref.1) | copy-start | bytes 3145732

commit v6 on v5

--- a/solution.py
+++ b/solution.py
@@ -13,6 +13,7 @@
 N = 4
 NB = 4
 STEP = 256
+PIECES = 2
 ORDER = [
     (0, 0, 0, 0, 0), (0, 0, 1, 0, 0), (0, 1, 0, 0, 0), (0, 0, 2, 0, 0), (0, 1, 1, 0, 0), (0, 0, 3, 0, 0),
     (0, 1, 2, 0, 0), (0, 2, 0, 0, 1), (0, 2, 0, 0, 0), (0, 1, 3, 0, 0), (0, 2, 1, 0, 0), (0, 2, 1, 0, 1),
@@ -345,13 +346,26 @@
         take(NB * rows, 2 * H, sent.at[4, stage])
 
 
+def store(refined_ref, cosample_ref, refined_out, cosample_out, sem):
+    size = refined_ref.shape[0] // PIECES
+    copies = [pltpu.make_async_copy(cosample_ref, cosample_out, sem.at[PIECES])]
+    for q in range(PIECES):
+        rows = pl.ds(q * size, size)
+        copies.append(pltpu.make_async_copy(refined_ref.at[rows], refined_out.at[rows], sem.at[q]))
+    for copy in copies:
+        copy.start()
+    for copy in copies:
+        copy.wait()
+
+
 def local(snapshots, sketch):
     (points, times), k = snapshots.shape, sketch.shape[1]
     chunk, width = points // N, times // NB
     half, sub, half_b = chunk // 2, chunk // 4, width // 2
     vmem = pl.BlockSpec(memory_space=pltpu.VMEM)
     sums = ((N, half), (N, 3, sub // 4), (N, sub // 2), (N, sub // 8), (N, 3, sub // 8))
-    return pl.pallas_call(
+    sketch = pltpu.with_memory_space_constraint(sketch, pltpu.HBM)
+    refined, cosample = pl.pallas_call(
         kernel,
         name="window",
         out_shape=[jax.ShapeDtypeStruct((points, k), F32), jax.ShapeDtypeStruct((times, k), F32)],
@@ -391,6 +405,16 @@
             flops=18 * points * times * k, bytes_accessed=4 * points * times, transcendentals=0
         ),
     )(snapshots, sketch)
+    hbm = pl.BlockSpec(memory_space=pl.ANY)
+    return pl.pallas_call(
+        store,
+        name="store",
+        out_shape=[jax.ShapeDtypeStruct((points, k), F32), jax.ShapeDtypeStruct((times, k), F32)],
+        in_specs=[vmem, vmem],
+        out_specs=[hbm, hbm],
+        scratch_shapes=[pltpu.SemaphoreType.DMA((PIECES + 1,))],
+        compiler_params=pltpu.CompilerParams(has_side_effects=True, vmem_limit_bytes=4 << 20),
+    )(refined, cosample)
 
 
 def solution(mesh):

time: 98.3 us -> 98.8 us (level)
  Pallas kernels: 94.1 us -> 97.9 us
  local copies, waits for them, and re-layouts: 3.51 us -> 0 us
    unnamed x4 -> x0, local copies, waits for them, and re-layouts: 3.51 us -> none
    pallas_call x1, Pallas kernels: 94.1 us -> 96.2 us  [local(): pl.pallas_call(kernel, name='window', out_shape=[jax.ShapeDtypeStruct((po...]
    pallas_call x0 -> x1, Pallas kernels: none -> 1.69 us  [local(): pl.pallas_call(store, name='store', out_shape=[jax.ShapeDtypeStruct((poin...]
where the time goes in v6:
time: 98.8 us; the launch traced here: 98.7 us
  Pallas kernels  97.9 us (99%)
    pallas_call x1, Pallas kernels, local(): pl.pallas_call(kernel, name='window', out_shape=[jax.ShapeDtypeStruct((po...  96.2 us

profile of v6, /device:TPU:1, one launch (start us, length us, event | category | flops | bytes accessed | tf_op | source)
XLA Modules:
  0.0 98.7 jit_solution(15619145226826915337)
XLA Ops:
  0.6 96.2 %window.1 = (f32[2048,256]{1,0:T(8,128)S(1)}, f32[1024,256]{1,0:T(8,128)S(1)}) custom-call(f32[2048,1024]{1,0:T(8,128)} %snap_ref.1, f32[1024,256]{1,0:T(8,128)} %sketch_ref.1), custom_call_target="tpu_custom_call" | custom-call | flops 9663676416 | bytes 8388608 | tf_op jit(solution)/shard_map/window/pallas_call | solution.py:368
  96.8 1.7 %store.1 = (f32[2048,256]{1,0:T(8,128)}, f32[1024,256]{1,0:T(8,128)}) custom-call(f32[2048,256]{1,0:T(8,128)S(1)} %get-tuple-element.4.refined_ref, f32[1024,256]{1,0:T(8,128)S(1)} %get-tuple-element.5.cosample_ref), custom_call_target="tpu_custom_call" | custom-call | tf_op jit(solution)/shard_map/store/pallas_call | solution.py:409

commit v7 on v6

--- a/solution.py
+++ b/solution.py
@@ -13,7 +13,7 @@
 N = 4
 NB = 4
 STEP = 256
-PIECES = 2
+PIECES = 4
 ORDER = [
     (0, 0, 0, 0, 0), (0, 0, 1, 0, 0), (0, 1, 0, 0, 0), (0, 0, 2, 0, 0), (0, 1, 1, 0, 0), (0, 0, 3, 0, 0),
     (0, 1, 2, 0, 0), (0, 2, 0, 0, 1), (0, 2, 0, 0, 0), (0, 1, 3, 0, 0), (0, 2, 1, 0, 0), (0, 2, 1, 0, 1),
@@ -102,8 +102,7 @@
 
     load_sketch = pltpu.make_async_copy(sketch_ref, sketch, sketch_sem)
     load_sketch.start()
-    for q in range(points // STEP):
-        load(q).start()
+    load(0).start()
 
     barrier = pltpu.get_barrier_semaphore()
     peers = [other_core, other_x, other_xh, *peer_y[1:], *peer_z[1:]]
@@ -217,6 +216,9 @@
         for start in range(i * chunk, (i + 1) * chunk, size):
             for q in range(start // STEP, (start + size) // STEP):
                 load(q).wait()
+                if q == 0:
+                    for later in range(2 * chunk // STEP, points // STEP):
+                        load(later).start()
             rows = pl.ds(start, size)
             high, low = split(wide[rows, :])
             s_hi[rows, :] = high
@@ -243,6 +245,8 @@
     def begin_1(i, h, p):
         if i == 0:
             load_sketch.wait()
+            for q in range(1, 2 * chunk // STEP):
+                load(q).start()
             b_hi[...], b_lo[...] = split(sketch[...])
         multiply_1(i)
         if i == 0:

time: 98.8 us -> 96.7 us (0.979)
  Pallas kernels: 97.9 us -> 95.8 us
    pallas_call x1, Pallas kernels: 96.2 us -> 94.1 us  [local(): pl.pallas_call(kernel, name='window', out_shape=[jax.ShapeDtypeStruct((po...]
where the time goes in v7:
time: 96.7 us; the launch traced here: 96.6 us
  Pallas kernels  95.8 us (99%)
    pallas_call x1, Pallas kernels, local(): pl.pallas_call(kernel, name='window', out_shape=[jax.ShapeDtypeStruct((po...  94.1 us

profile of v7, /device:TPU:1, one launch (start us, length us, event | category | flops | bytes accessed | tf_op | source)
XLA Modules:
  0.0 96.6 jit_solution(5305523661963993717)
XLA Ops:
  0.6 94.1 %window.1 = (f32[2048,256]{1,0:T(8,128)S(1)}, f32[1024,256]{1,0:T(8,128)S(1)}) custom-call(f32[2048,1024]{1,0:T(8,128)} %snap_ref.1, f32[1024,256]{1,0:T(8,128)} %sketch_ref.1), custom_call_target="tpu_custom_call" | custom-call | flops 9663676416 | bytes 8388608 | tf_op jit(solution)/shard_map/window/pallas_call | solution.py:372
  94.7 1.7 %store.1 = (f32[2048,256]{1,0:T(8,128)}, f32[1024,256]{1,0:T(8,128)}) custom-call(f32[2048,256]{1,0:T(8,128)S(1)} %get-tuple-element.4.refined_ref, f32[1024,256]{1,0:T(8,128)S(1)} %get-tuple-element.5.cosample_ref), custom_call_target="tpu_custom_call" | custom-call | tf_op jit(solution)/shard_map/store/pallas_call | solution.py:413

commit v8 on v7

--- a/solution.py
+++ b/solution.py
@@ -97,7 +97,10 @@
     piece = half_b // NZ
 
     def load(q):
-        rows = pl.ds(q * STEP, STEP)
+        start = q * STEP
+        if q < 2:
+            start = pl.multiple_of((1 - core if q == 0 else core) * STEP, STEP)
+        rows = pl.ds(start, STEP)
         return pltpu.make_async_copy(snap_ref.at[rows], wide.at[rows], load_sem.at[q])
 
     load_sketch = pltpu.make_async_copy(sketch_ref, sketch, sketch_sem)
@@ -211,19 +214,11 @@
 
         return start, spread, to_core, arrive
 
-    def multiply_1(i):
-        size = STEP if i == 0 else chunk
-        for start in range(i * chunk, (i + 1) * chunk, size):
-            for q in range(start // STEP, (start + size) // STEP):
-                load(q).wait()
-                if q == 0:
-                    for later in range(2 * chunk // STEP, points // STEP):
-                        load(later).start()
-            rows = pl.ds(start, size)
-            high, low = split(wide[rows, :])
-            s_hi[rows, :] = high
-            s_lo[rows, :] = low
-            part[rows, :] = dot(high, b_hi[...]) + (dot(high, b_lo[...]) + dot(low, b_hi[...]))
+    def multiply_1(rows):
+        high, low = split(wide[rows, :])
+        s_hi[rows, :] = high
+        s_lo[rows, :] = low
+        part[rows, :] = dot(high, b_hi[...]) + (dot(high, b_lo[...]) + dot(low, b_hi[...]))
 
     def add_back(i, h):
         rows = pl.ds(i * chunk, chunk)
@@ -248,10 +243,19 @@
             for q in range(1, 2 * chunk // STEP):
                 load(q).start()
             b_hi[...], b_lo[...] = split(sketch[...])
-        multiply_1(i)
-        if i == 0:
+            load(0).wait()
+            for q in range(2 * chunk // STEP, points // STEP):
+                load(q).start()
+            multiply_1(pl.ds(pl.multiple_of((1 - core) * STEP, STEP), STEP))
             pl.semaphore_wait(barrier, len(peers))
-        first_1(i)
+            first_1(i)
+            load(1).wait()
+            multiply_1(pl.ds(pl.multiple_of(core * STEP, STEP), STEP))
+        else:
+            for q in range(i * chunk // STEP, (i + 1) * chunk // STEP):
+                load(q).wait()
+            multiply_1(pl.ds(i * chunk, chunk))
+            first_1(i)
 
     def finish_1(i, h, p):
         if h == 0:

time: 96.7 us -> 96.7 us (level)
  no operation moved by 1% of the time
where the time goes in v8:
time: 96.7 us; the launch traced here: 96.6 us
  Pallas kernels  95.8 us (99%)
    pallas_call x1, Pallas kernels, local(): pl.pallas_call(kernel, name='window', out_shape=[jax.ShapeDtypeStruct((po...  94.1 us

profile of v8, /device:TPU:1, one launch (start us, length us, event | category | flops | bytes accessed | tf_op | source)
XLA Modules:
  0.0 96.6 jit_solution(3263225636633526811)
XLA Ops:
  0.6 94.1 %window.1 = (f32[2048,256]{1,0:T(8,128)S(1)}, f32[1024,256]{1,0:T(8,128)S(1)}) custom-call(f32[2048,1024]{1,0:T(8,128)} %snap_ref.1, f32[1024,256]{1,0:T(8,128)} %sketch_ref.1), custom_call_target="tpu_custom_call" | custom-call | flops 9663676416 | bytes 8388608 | tf_op jit(solution)/shard_map/window/pallas_call | solution.py:376
  94.8 1.7 %store.1 = (f32[2048,256]{1,0:T(8,128)}, f32[1024,256]{1,0:T(8,128)}) custom-call(f32[2048,256]{1,0:T(8,128)S(1)} %get-tuple-element.4.refined_ref, f32[1024,256]{1,0:T(8,128)S(1)} %get-tuple-element.5.cosample_ref), custom_call_target="tpu_custom_call" | custom-call | tf_op jit(solution)/shard_map/store/pallas_call | solution.py:417
